TPU v7x, 256 devices: a whole 4x4x8 slice. The times are simulated.
256 devices in a mesh: op: 32 (over y, x, core), grp: 8 (over z).
Axes of the slice: x: 4, y: 4, z: 8, core: 2. Of those that a mesh axis runs over, the one named last changes fastest.
Arguments:
- wavefunction: bfloat16 [8, 256, 256], P('grp'), may hold values from -6 to 6
- block_rows: int32 [8], P('grp'), may hold values from 128 to 256
- left_terms: bfloat16 [12288, 256, 256], P(('op', 'grp')), may hold values from -0.375 to 0.375
- right_terms: bfloat16 [12288, 256, 256], P(('op', 'grp')), may hold values from -0.013671875 to 0.013671875
- block_pairs: int32 [12288, 2], P(('op', 'grp')), may hold values from 0 to 7
- live_counts: int32 [256], P(('op', 'grp')), may hold values from 1 to 48, 6144 in all
Outputs:
- sigma: float32 [8, 256, 256], P('grp', 'op')
Inputs may be any that keep to these rules, and one draw needn't show every extreme that they name: `live_counts`: some device uses all 48 of its slots.
All inputs are finite; a program needn't handle non-finite values.
Results may differ from a plain program's by a relative error of at most 0.0029.
Values may be sent and summed in bfloat16 or wider, within the bound.
No kernel may reach another device: no remote copies, remote signals or barrier semaphores. Data moves between devices by JAX's collectives and lax.ppermute only.
A program may use at most 128 MiB of HBM per device.

v0:
```python
import jax
import jax.numpy as jnp
from jax import lax
from jax.sharding import PartitionSpec as P


def body(wavefunction, block_rows, left_terms, right_terms, block_pairs, live_counts):
    block_count, left_dim, right_dim = wavefunction.shape
    row_index = lax.broadcasted_iota(jnp.int32, (block_count, left_dim, 1), 1)
    masked = jnp.where(
        row_index < block_rows[:, None, None], wavefunction, jnp.zeros_like(wavefunction)
    )
    everyone = lax.all_gather(masked, "grp", axis=0, tiled=True)
    all_blocks = everyone.shape[0]
    slot_count = left_terms.shape[0]
    slot_live = lax.broadcasted_iota(jnp.int32, (slot_count,), 0) < live_counts[0]
    sources = jnp.take(everyone, block_pairs[:, 0], axis=0)
    left_product = jnp.einsum(
        "kij,kjc->kic", left_terms, sources, preferred_element_type=jnp.float32
    ).astype(jnp.bfloat16)
    contributions = jnp.einsum(
        "kic,kcd->kid", left_product, right_terms, preferred_element_type=jnp.float32
    )
    contributions = contributions.reshape(slot_count, left_dim * right_dim)
    targets = jnp.where(slot_live, block_pairs[:, 1], jnp.int32(-1))
    wanted = lax.broadcasted_iota(jnp.int32, (all_blocks, slot_count), 0)
    selector = (targets[None, :] == wanted).astype(jnp.float32)
    summed = jnp.dot(
        selector, contributions, precision=lax.Precision.HIGHEST, preferred_element_type=jnp.float32
    )
    all_sums = summed.reshape(all_blocks, left_dim, right_dim)
    shares = lax.psum_scatter(all_sums, "op", scatter_dimension=1, tiled=True)
    shares = lax.psum_scatter(shares, "grp", scatter_dimension=0, tiled=True)
    rows_here = shares.shape[1]
    own_rows = lax.axis_index("op") * rows_here + lax.broadcasted_iota(
        jnp.int32, (block_count, rows_here, 1), 1
    )
    return jnp.where(own_rows < block_rows[:, None, None], shares, jnp.zeros_like(shares))


def solution(mesh):
    placed = (
        P("grp", None, None),
        P("grp"),
        P(("op", "grp"), None, None),
        P(("op", "grp"), None, None),
        P(("op", "grp"), None),
        P(("op", "grp")),
    )
    return jax.shard_map(
        body, mesh=mesh, in_specs=placed, out_specs=P("grp", "op", None), check_vma=False
    )
```

profile of v0, /device:TPU:2, one launch (start us, length us, event | category | flops | bytes accessed | tf_op | source)
XLA Modules:
  0.0 215.6 jit_solution(196053515932141834)
XLA Ops:
  6.5 0.0 all-gather.2.cloned.1.call-start
  7.2 1.7 broadcast_select_fusion
  8.9 0.0 all-gather.2.cloned.1.call-update
  8.9 0.0 reduce-scatter.3.cloned.1.call-start
  9.6 0.7 fusion.19
  10.3 0.7 and_bitcast_fusion
  11.0 0.7 compare_select_fusion.1
  11.6 39.2 %all-gather.2.cloned.1.call-done = bf16[8,256,256]{2,1,0:T(8,128)(2,1)} async-done(((bf16[1,256,256]{2,1,0:T(8,128)(2,1)}), bf16[8,256,256]{2,1,0:T(8,128)(2,1)}) %all-gather.2.cloned.1.call-update) | async-done | bytes 1048592 | tf_op jit(solution)/shard_map/all_gather | solution.py:13
  50.9 6.1 %gather_fusion = bf16[48,256,256]{2,1,0:T(8,128)(2,1)} fusion(bf16[8,256,256]{2,1,0:T(8,128)(2,1)} %all-gather.2.cloned.1.call-done, s32[1024]{0:T(1024)S(1)} %pad_clamp_fusion), kind=kCustom, calls=%fused_computation | custom fusion | bytes 12583104 | tf_op jit(solution)/shard_map/jit(_take)/gather | solution.py:17
  56.9 11.1 %fusion.3 = f32[48,256,256]{2,1,0:T(8,128)} fusion(bf16[48,256,256]{2,1,0:T(8,128)(2,1)} %param.9, bf16[48,256,256]{2,1,0:T(8,128)(2,1)} %param.8, bf16[48,256,256]{2,1,0:T(8,128)(2,1)} %gather_fusion, pred[48]{0:T(512)(128)(4,1)S(1)} %and_bitcast_fusion), kind=kOutput, calls=%fused_computation.4 | convolution fusion | flops 3227516928 | bytes 31457328 | tf_op jit(solution)/shard_map/kic,kcd->kid/dot_general | solution.py:21
  68.0 16.3 %fusion = f32[8,256,256]{2,0,1:T(8,128)} fusion(s32[48]{0:T(128)S(1)} %compare_select_fusion.1, f32[6,8,256,256]{3,2,1,0:T(8,128)} %bitcast.27), kind=kOutput, calls=%fused_computation.1 | convolution fusion | flops 301990272 | bytes 14680256 | tf_op jit(solution)/shard_map/dot_general | solution.py:28
  84.2 0.0 reduce-scatter.3.cloned.1.call-update
  84.3 0.0 reduce-scatter.5.cloned.1.call-start
  84.3 84.7 %reduce-scatter.3.cloned.1.call-done = f32[8,8,256]{2,0,1:T(8,128)} async-done(((f32[8,256,256]{2,0,1:T(8,128)}), f32[8,8,256]{2,0,1:T(8,128)}) %reduce-scatter.3.cloned.1.call-update) | async-done | bytes 65552 | tf_op jit(solution)/shard_map/reduce_scatter | solution.py:32
  169.1 1.5 copy.13
  170.5 0.0 reduce-scatter.5.cloned.1.call-update
  170.6 37.1 %reduce-scatter.5.cloned.1.call-done = f32[1,8,256]{2,1,0:T(8,128)} async-done(((f32[8,8,256]{2,1,0:T(8,128)}), f32[1,8,256]{2,1,0:T(8,128)}) %reduce-scatter.5.cloned.1.call-update) | async-done | bytes 8208 | tf_op jit(solution)/shard_map/reduce_scatter | solution.py:33
  207.7 1.4 broadcast_select_fusion.1
  (3 shorter events, 0.0 us)
Async XLA Ops:
  6.5 44.3 %all-gather.2.cloned.1.call-start = ((), (), s32[]{:S(2)}) async-start(), calls=%async_computation.2 | async-start | bytes 1179648 | tf_op jit(solution)/shard_map/all_gather | solution.py:13
  8.9 160.2 %reduce-scatter.3.cloned.1.call-start = ((), (), s32[]{:S(2)}) async-start(), calls=%async_computation.3 | async-start | bytes 2162688 | tf_op jit(solution)/shard_map/reduce_scatter | solution.py:32
  84.3 123.4 %reduce-scatter.5.cloned.1.call-start = ((), (), s32[]{:S(2)}) async-start(), calls=%async_computation.4 | async-start | bytes 73728 | tf_op jit(solution)/shard_map/reduce_scatter | solution.py:33
Sparse Core Ops, SparseCore 0:
  9.1 41.6 all-gather.1
  84.4 84.6 reduce-scatter.2
  171.6 36.1 reduce-scatter.4
where the time goes:
time: 216 us
  waiting for transfers between devices  161 us (75%)
  matrix products  27.3 us (13%)
  between operations  14.4 us (7%)
  local copies, waits for them, and re-layouts  7.54 us (3%)
  other arithmetic  5.09 us (2%)
    reduce_scatter x1, waiting for transfers between devices, body(): shares = lax.psum_scatter(all_sums, 'op', scatter_dimension=1, tiled=True)  84.7 us
    all_gather x1, waiting for transfers between devices, body(): everyone = lax.all_gather(masked, 'grp', axis=0, tiled=True)  39.2 us
    reduce_scatter x1, waiting for transfers between devices, body(): shares = lax.psum_scatter(shares, 'grp', scatter_dimension=0, tiled=True)  37.1 us
    dot_general x1, matrix products, body(): jnp.dot(selector, contributions, precision=lax.Precision.HIGHEST, preferr...  16.3 us
    dot_general x1, matrix products, body(): jnp.einsum('kic,kcd->kid', left_product, right_terms, preferred_element_t...  11.1 us
    gather x1, local copies, waits for them, and re-layouts, body(): sources = jnp.take(everyone, block_pairs[:, 0], axis=0)  6.06 us
  transfers between devices with their start and end apart: 3, of which 3 were waited for; matrix products, arithmetic and copies ran while one was open for 1% of the time, Pallas kernels for 0%

commit v1 on v0

v1 whole, which is shorter than its diff:
```python
import jax
import jax.numpy as jnp
from jax import lax
from jax.experimental import pallas as pl
from jax.experimental.pallas import tpu as pltpu
from jax.sharding import Mesh, PartitionSpec as P

GROUP = 8
LAYER = ("y", "x")
SWAP = [(0, 1), (1, 0)]


def term_kernel(
    core_ref, live_ref, pairs_ref, mine_ref, other_ref, left, right, keep_ref, send_ref,
    psi, acc, psi_sem, out_sem,
):
    core, live = core_ref[0], live_ref[0]
    blocks, half, width = mine_ref.shape
    tiles, share, _ = send_ref.shape
    mine_rows = pl.ds(pl.multiple_of(core * half, half), half)
    other_rows = pl.ds(pl.multiple_of((1 - core) * half, half), half)
    loads = [
        pltpu.make_async_copy(mine_ref, psi.at[:, mine_rows], psi_sem.at[0]),
        pltpu.make_async_copy(other_ref, psi.at[:, other_rows], psi_sem.at[1]),
    ]
    for load in loads:
        load.start()
    acc[...] = jnp.zeros_like(acc)
    for load in loads:
        load.wait()

    def step(j, carry):
        products = []
        for i in range(GROUP):
            k = j * GROUP + i
            product = jnp.dot(left[k], psi[pairs_ref[k, 0]], preferred_element_type=jnp.float32)
            products.append(product.astype(jnp.bfloat16))
        for i in range(GROUP):
            k = j * GROUP + i
            target = jnp.where(k < live, pairs_ref[k, 1], blocks)
            term = jnp.dot(products[i], right[k], preferred_element_type=jnp.float32)
            term = term.reshape(tiles, 2, 8, width)
            for c in range(2):
                acc[c, :, target] += term[:, c]
        return carry

    lax.fori_loop(0, (live + GROUP - 1) // GROUP, step, 0)
    for tile in range(tiles):
        sums = acc[1 - core, tile, :blocks].reshape(share, width)
        send_ref[tile] = sums.astype(send_ref.dtype)
    keep = pltpu.make_async_copy(acc.at[core, :, :blocks], keep_ref, out_sem)
    keep.start()
    keep.wait()


def term_sums(core, live, pairs, mine, other, left, right):
    slots, rows, width = left.shape
    blocks = mine.shape[0]
    tiles = rows // 16
    smem = pl.BlockSpec(memory_space=pltpu.SMEM)
    vmem = pl.BlockSpec(memory_space=pltpu.VMEM)
    anywhere = pl.BlockSpec(memory_space=pl.ANY)
    return pl.pallas_call(
        term_kernel,
        out_shape=(
            jax.ShapeDtypeStruct((tiles, blocks, 8, width), jnp.float32),
            jax.ShapeDtypeStruct((tiles, blocks * 8, width), jnp.bfloat16),
        ),
        in_specs=[smem, smem, smem, anywhere, anywhere, vmem, vmem],
        out_specs=(anywhere, vmem),
        scratch_shapes=[
            pltpu.VMEM((blocks, rows, width), jnp.bfloat16),
            pltpu.VMEM((2, tiles, blocks + 1, 8, width), jnp.float32),
            pltpu.SemaphoreType.DMA((2,)),
            pltpu.SemaphoreType.DMA,
        ],
        compiler_params=pltpu.CompilerParams(vmem_limit_bytes=24 * 1024 * 1024),
        cost_estimate=pl.CostEstimate(
            flops=4 * rows * rows * width * slots,
            bytes_accessed=4 * rows * width * slots,
            transcendentals=0,
        ),
    )(core, live, pairs, mine, other, left, right)


def body(wavefunction, block_rows, left_terms, right_terms, block_pairs, live_counts):
    _, rows, width = wavefunction.shape
    core = lax.axis_index("c").astype(jnp.int32)
    blocks = lax.axis_size("z")
    half = rows // 2
    own_half = lax.dynamic_slice_in_dim(wavefunction[0], core * half, half, 0)
    row_index = core * half + lax.broadcasted_iota(jnp.int32, (half, 1), 0)
    masked = jnp.where(row_index < block_rows[0], own_half, jnp.zeros_like(own_half))
    mine = lax.all_to_all(jnp.broadcast_to(masked, (blocks, half, width)), "z", 0, 0)
    other = lax.ppermute(mine, "c", SWAP)
    keep, send = term_sums(
        core[None], live_counts, block_pairs, mine, other, left_terms, right_terms
    )
    received = lax.ppermute(send, "c", SWAP)
    tiles = keep.shape[0]
    pair_sum = keep.reshape(tiles, blocks * 8, width) + received.astype(jnp.float32)
    pieces = lax.all_to_all(pair_sum.astype(jnp.bfloat16), LAYER, 0, 0)
    layer_sum = pieces.astype(jnp.float32).sum(0).reshape(blocks, 8, width)
    sigma = lax.all_to_all(layer_sum, "z", 0, 0).sum(0)
    own_tile = lax.axis_index(("y", "x", "c"))
    own_rows = own_tile * 8 + lax.broadcasted_iota(jnp.int32, (8, 1), 0)
    return jnp.where(own_rows < block_rows[0], sigma, jnp.zeros_like(sigma))[None]


def solution(mesh):
    devices = mesh.devices.reshape(4, 4, 2, mesh.shape["grp"])
    grid = Mesh(devices, ("y", "x", "c", "z"))
    everywhere = ("y", "x", "c", "z")
    placed = (
        P("z", None, None),
        P("z"),
        P(everywhere, None, None),
        P(everywhere, None, None),
        P(everywhere, None),
        P(everywhere),
    )
    return jax.shard_map(
        body, mesh=grid, in_specs=placed, out_specs=P("z", ("y", "x", "c"), None), check_vma=False
    )
```

time: 216 us -> 73.8 us (0.34)
  waiting for transfers between devices: 161 us -> 10.6 us
  blocking collectives: 0 us -> 44.8 us
  matrix products: 27.3 us -> 0 us
  between operations: 14.4 us -> 1.39 us
  Pallas kernels: 0 us -> 3.72 us
  starting transfers between devices: 0.09 us -> 3.44 us
  other arithmetic: 5.09 us -> 2.48 us
    reduce_scatter x2 -> x0, waiting for transfers between devices: 122 us -> none  [the longest x1 84.7 us: body(): shares = lax.psum_scatter(all_sums, 'op', scatter_dimension=1, tiled=True)]
    all_to_all x0 -> x2, blocking collectives: none -> 44.8 us  [the longest x1 25.8 us: body(): lax.all_to_all(jnp.broadcast_to(masked, (blocks, half, width)), 'z', 0, 0)]
    all_gather x1 -> x0, waiting for transfers between devices: 39.2 us -> none  [body(): everyone = lax.all_gather(masked, 'grp', axis=0, tiled=True)]
    dot_general x2 -> x0, matrix products: 27.3 us -> none  [the longest x1 16.3 us: body(): jnp.dot(selector, contributions, precision=lax.Precision.HIGHEST, preferr...]
    all_to_all x0 -> x1, waiting for transfers between devices: none -> 8.26 us  [body(): sigma = lax.all_to_all(layer_sum, 'z', 0, 0).sum(0)]
    unnamed x0 -> x5, local copies, waits for them, and re-layouts: none -> 6.34 us
    gather x1 -> x0, local copies, waits for them, and re-layouts: 6.06 us -> none  [body(): sources = jnp.take(everyone, block_pairs[:, 0], axis=0)]
    pallas_call x0 -> x1, Pallas kernels: none -> 3.72 us  [term_sums(): pl.pallas_call(term_kernel, out_shape=(jax.ShapeDtypeStruct((tiles, block...]
where the time goes in v1:
time: 73.8 us; the launch traced here: 72.8 us
  blocking collectives  44.8 us (61%)
  waiting for transfers between devices  10.6 us (14%)
  local copies, waits for them, and re-layouts  6.37 us (9%)
  Pallas kernels  3.72 us (5%)
  starting transfers between devices  3.44 us (5%)
  other arithmetic  2.48 us (3%)
  between operations  1.39 us (2%)
    all_to_all x1, blocking collectives, body(): lax.all_to_all(jnp.broadcast_to(masked, (blocks, half, width)), 'z', 0, 0)  25.8 us
    all_to_all x1, blocking collectives, body(): pieces = lax.all_to_all(pair_sum.astype(jnp.bfloat16), LAYER, 0, 0)  19 us
    all_to_all x1, waiting for transfers between devices, body(): sigma = lax.all_to_all(layer_sum, 'z', 0, 0).sum(0)  8.26 us
    unnamed x5, local copies, waits for them, and re-layouts  6.34 us
    pallas_call x1, Pallas kernels, term_sums(): pl.pallas_call(term_kernel, out_shape=(jax.ShapeDtypeStruct((tiles, block...  3.72 us
    all_to_all x1, starting transfers between devices, body(): sigma = lax.all_to_all(layer_sum, 'z', 0, 0).sum(0)  3.35 us
    ppermute x1, waiting for transfers between devices, body(): received = lax.ppermute(send, 'c', SWAP)  1.9 us
  transfers between devices with their start and end apart: 3, of which 3 were waited for; matrix products, arithmetic and copies ran while one was open for 1% of the time, Pallas kernels for 0%

profile of v1, /device:TPU:2, one launch (start us, length us, event | category | flops | bytes accessed | tf_op | source)
XLA Modules:
  0.0 72.8 jit_solution(770963105778893203)
XLA Ops:
  0.7 0.9 %bitcast_select_fusion = bf16[128,256]{1,0:T(8,128)(2,1)S(1)} fusion(bf16[1,256,256]{2,1,0:T(8,128)(2,1)} %param.6, s32[]{:T(128)S(6)} %select_n.18, pred[128]{0:T(512)(128)(4,1)S(1)} %add_compare_fusion), kind=kLoop, calls=%fused_computation.3 | loop fusion | flops 32768 | bytes 131204 | tf_op jit(solution)/shard_map/jit(_where)/select_n | solution.py:93
  1.6 25.8 %all_to_all.15.mine_ref = bf16[8,128,256]{2,1,0:T(8,128)(2,1)S(1)} all-to-all(bf16[8,128,256]{2,1,0:T(8,128)(2,1)S(1)} %broadcast_in_dim.33), channel_id=1, replica_groups=mesh['y'=4,'x'=4,'c'=2,'z'=8] {'z'}, dimensions={0} | all-to-all | bytes 1048576 | tf_op jit(solution)/shard_map/all_to_all | solution.py:94
  27.4 0.0 collective-permute-start
  28.1 0.8 %copy.8.pairs_ref = s32[48,2]{1,0:T(8,128)S(1)} copy(s32[48,2]{0,1:T(2,128)} %param.10) | data formatting | bytes 768 | tf_op args[4]
  28.8 0.5 collective-permute-done.other_ref
  29.3 0.0 copy-start
  29.3 2.8 %copy-done = bf16[48,256,256]{2,1,0:T(8,128)(2,1)S(1)} copy-done((bf16[48,256,256]{2,1,0:T(8,128)(2,1)S(1)}, bf16[48,256,256]{2,1,0:T(8,128)(2,1)}, u32[]{:S(2)}) %copy-start) | copy-done | bytes 6291480
  32.1 0.0 copy-start.1
  32.1 2.8 %copy-done.1 = bf16[48,256,256]{2,1,0:T(8,128)(2,1)S(1)} copy-done((bf16[48,256,256]{2,1,0:T(8,128)(2,1)S(1)}, bf16[48,256,256]{2,1,0:T(8,128)(2,1)}, u32[]{:S(2)}) %copy-start.1) | copy-done | bytes 6291480
  34.9 3.7 %shard_map.64 = (f32[16,8,8,256]{3,2,1,0:T(8,128)S(1)}, bf16[16,64,256]{2,1,0:T(8,128)(2,1)S(1)}) custom-call(s32[1]{0:T(128)} %bitcast.1.core_ref, s32[1]{0:T(128)S(6)} %copy.10.live_ref, s32[48,2]{1,0:T(8,128)S(1)} %copy.8.pairs_ref, bf16[8,128,256]{2,1,0:T(8,128)(2,1)S(1)} %all_to_all.15.mine_ref, ...), custom_call_target="tpu_custom_call" | custom-call | flops 3221225472 | bytes 12582912 | tf_op jit(solution)/shard_map/pallas_call | solution.py:63
  38.6 0.1 collective-permute-start.1
  38.7 1.9 %collective-permute-done.1 = bf16[16,64,256]{2,1,0:T(8,128)(2,1)S(1)} collective-permute-done((bf16[16,64,256]{2,1,0:T(8,128)(2,1)S(1)}, bf16[16,64,256]{2,1,0:T(8,128)(2,1)S(1)}, u32[]{:S(2)}, u32[]{:S(2)}) %collective-permute-start.1) | collective-permute-done | bytes 524320 | tf_op jit(solution)/shard_map/ppermute | solution.py:99
  40.6 0.2 fusion
  40.8 19.0 %all_to_all.16 = bf16[16,64,256]{2,1,0:T(8,128)(2,1)S(1)} all-to-all(bf16[16,64,256]{2,1,0:T(8,128)(2,1)S(1)} %fusion), channel_id=1, replica_groups=mesh['y'=4,'x'=4,'c'=2,'z'=8] {'y','x'}, dimensions={0} | all-to-all | bytes 1048576 | tf_op jit(solution)/shard_map/all_to_all | solution.py:102
  59.8 0.7 convert_reduce_fusion
  60.5 3.3 %all-to-all-start.2 = ((f32[8,8,256]{2,1,0:T(8,128)}), f32[8,8,256]{2,1,0:T(8,128)S(1)}, u32[]{:S(2)}, u32[]{:S(2)}) async-start(f32[8,8,256]{2,1,0:T(8,128)} %bitcast.4), calls=%async_computation.2 | async-start | bytes 131072 | tf_op jit(solution)/shard_map/all_to_all | solution.py:104
  63.9 8.3 %all-to-all-done.2 = f32[8,8,256]{2,1,0:T(8,128)S(1)} async-done(((f32[8,8,256]{2,1,0:T(8,128)}), f32[8,8,256]{2,1,0:T(8,128)S(1)}, u32[]{:S(2)}, u32[]{:S(2)}) %all-to-all-start.2) | async-done | bytes 65568 | tf_op jit(solution)/shard_map/all_to_all | solution.py:104
  72.2 0.7 bitcast_select_fusion.1
  (4 shorter events, 0.1 us)
Async XLA Ops:
  27.4 1.9 %collective-permute-start = (bf16[8,128,256]{2,1,0:T(8,128)(2,1)S(1)}, bf16[8,128,256]{2,1,0:T(8,128)(2,1)S(1)}, u32[]{:S(2)}, u32[]{:S(2)}) collective-permute-start(bf16[8,128,256]{2,1,0:T(8,128)(2,1)S(1)} %all_to_all.15.mine_ref), channel_id=1, source_target_pairs={{0,8},{8,0},{1,9},{9,1},{2,10},{10,2},{3,11},{11,3},{4,12},{12,4},... | collective-permute-start | bytes 1572872 | tf_op jit(solution)/shard_map/ppermute | solution.py:95
  29.3 2.8 %copy-start = (bf16[48,256,256]{2,1,0:T(8,128)(2,1)S(1)}, bf16[48,256,256]{2,1,0:T(8,128)(2,1)}, u32[]{:S(2)}) copy-start(bf16[48,256,256]{2,1,0:T(8,128)(2,1)} %left.1) | copy-start | bytes 18874372
  32.1 2.8 %copy-start.1 = (bf16[48,256,256]{2,1,0:T(8,128)(2,1)S(1)}, bf16[48,256,256]{2,1,0:T(8,128)(2,1)}, u32[]{:S(2)}) copy-start(bf16[48,256,256]{2,1,0:T(8,128)(2,1)} %right.1) | copy-start | bytes 18874372
  38.6 2.0 %collective-permute-start.1 = (bf16[16,64,256]{2,1,0:T(8,128)(2,1)S(1)}, bf16[16,64,256]{2,1,0:T(8,128)(2,1)S(1)}, u32[]{:S(2)}, u32[]{:S(2)}) collective-permute-start(bf16[16,64,256]{2,1,0:T(8,128)(2,1)S(1)} %get-tuple-element.8), channel_id=1, source_target_pairs={{0,8},{8,0},{1,9},{9,1},{2,10},{10,2},{3,11},{11,3},{4,12},{12,4},... | collective-permute-start | bytes 1572872 | tf_op jit(solution)/shard_map/ppermute | solution.py:99
  60.5 11.6 %all-to-all-start.2 = ((f32[8,8,256]{2,1,0:T(8,128)}), f32[8,8,256]{2,1,0:T(8,128)S(1)}, u32[]{:S(2)}, u32[]{:S(2)}) async-start(f32[8,8,256]{2,1,0:T(8,128)} %bitcast.4), calls=%async_computation.2 | async-start | bytes 131072 | tf_op jit(solution)/shard_map/all_to_all | solution.py:104

commit v2 on v1

v2 whole, which is shorter than its diff:
```python
import jax
import jax.numpy as jnp
from jax import lax
from jax.experimental import pallas as pl
from jax.experimental.pallas import tpu as pltpu
from jax.sharding import Mesh, PartitionSpec as P

GROUP = 8
PARTS = 4
LAYER = ("y", "x")
SWAP = [(0, 1), (1, 0)]
SMEM = pl.BlockSpec(memory_space=pltpu.SMEM)
VMEM = pl.BlockSpec(memory_space=pltpu.VMEM)


def prepare_kernel(
    place_ref, live_ref, pairs_ref, left_ref, right_ref,
    lists_ref, counts_ref, left_here, right_here, left_sem, right_sem,
):
    part = left_ref.shape[0] // PARTS
    loads = []
    for i in range(PARTS):
        slots = pl.ds(i * part, part)
        loads.append(
            pltpu.make_async_copy(left_ref.at[slots], left_here.at[slots], left_sem.at[i])
        )
        loads.append(
            pltpu.make_async_copy(right_ref.at[slots], right_here.at[slots], right_sem.at[i])
        )
    for load in loads:
        load.start()
    core, layer = place_ref[0], place_ref[1]

    def clear(i, carry):
        for which in range(2):
            lists_ref[which, 0, i] = 0
            lists_ref[which, 1, i] = 0
            lists_ref[which, 2, i] = 8
        return carry

    lax.fori_loop(0, lists_ref.shape[2], clear, 0)

    def place(k, counts):
        ahead = (pairs_ref[0, k] - layer) & 7
        hops = jnp.minimum(ahead, 8 - ahead)
        behind = (ahead > 4).astype(jnp.int32)
        theirs = jnp.where(hops == 0, 0, jnp.where(hops == 4, 1, 1 - (behind ^ core)))
        at = jnp.where(theirs == 0, counts[0], counts[1])
        lists_ref[theirs, 0, at] = k
        lists_ref[theirs, 1, at] = jnp.where(hops == 0, 0, 4 - hops)
        lists_ref[theirs, 2, at] = pairs_ref[1, k]
        return counts[0] + 1 - theirs, counts[1] + theirs

    first, second = lax.fori_loop(0, live_ref[0], place, (jnp.int32(0), jnp.int32(0)))
    counts_ref[0] = first
    counts_ref[1] = second
    for load in loads:
        load.wait()


def prepare(place, live, pairs, left, right):
    slots = pairs.shape[1]
    return pl.pallas_call(
        prepare_kernel,
        out_shape=(
            jax.ShapeDtypeStruct((2, 3, slots + GROUP), jnp.int32),
            jax.ShapeDtypeStruct((2,), jnp.int32),
            jax.ShapeDtypeStruct(left.shape, left.dtype),
            jax.ShapeDtypeStruct(right.shape, right.dtype),
        ),
        in_specs=[SMEM] * 3 + [pl.BlockSpec(memory_space=pl.ANY)] * 2,
        out_specs=(SMEM, SMEM, VMEM, VMEM),
        scratch_shapes=[pltpu.SemaphoreType.DMA((PARTS,)), pltpu.SemaphoreType.DMA((PARTS,))],
        compiler_params=pltpu.CompilerParams(vmem_limit_bytes=40 * 1024 * 1024),
        cost_estimate=pl.CostEstimate(
            flops=0, bytes_accessed=4 * (left.size + right.size), transcendentals=0
        ),
    )(place, live, pairs, left, right)


def add_terms(which, lists_ref, counts_ref, psi, left, right, acc):
    tiles, width = acc.shape[1], acc.shape[-1]

    def step(j, carry):
        products = []
        for i in range(GROUP):
            slot, source = lists_ref[which, 0, j * GROUP + i], lists_ref[which, 1, j * GROUP + i]
            block = psi[pl.ds(pl.multiple_of(source * width, width), width)]
            product = jnp.dot(left[slot], block, preferred_element_type=jnp.float32)
            products.append(product.astype(jnp.bfloat16))
        for i in range(GROUP):
            slot, target = lists_ref[which, 0, j * GROUP + i], lists_ref[which, 2, j * GROUP + i]
            term = jnp.dot(products[i], right[slot], preferred_element_type=jnp.float32)
            term = term.reshape(tiles, 2, 8, width)
            for c in range(2):
                acc[c, :, target] += term[:, c]
        return carry

    lax.fori_loop(0, (counts_ref[which] + GROUP - 1) // GROUP, step, 0)


def first_kernel(lists_ref, counts_ref, mine, left, right, acc):
    acc[...] = jnp.zeros_like(acc)
    add_terms(0, lists_ref, counts_ref, mine, left, right, acc)


def second_kernel(
    place_ref, lists_ref, counts_ref, mine, other, left, right, before, keep_ref, send_ref, psi, acc
):
    core = place_ref[0]
    tiles, share, width = send_ref.shape
    fetched, half = 4 * width, width // 2
    psi[width:fetched] = other[width:fetched]
    own_rows = pl.ds(pl.multiple_of(core * half, half), half)
    their_rows = pl.ds(pl.multiple_of((1 - core) * half, half), half)
    psi[own_rows] = mine[fetched : fetched + half]
    psi[their_rows] = other[fetched : fetched + half]
    acc[...] = before[...]
    add_terms(1, lists_ref, counts_ref, psi, left, right, acc)
    for tile in range(tiles):
        keep_ref[tile] = acc[core, tile, :8].reshape(share, width)
        send_ref[tile] = acc[1 - core, tile, :8].reshape(share, width).astype(send_ref.dtype)


def term_cost(left):
    slots, rows, width = left.shape
    return pl.CostEstimate(
        flops=2 * rows * rows * width * slots,
        bytes_accessed=2 * rows * width * slots,
        transcendentals=0,
    )


def first_terms(lists, counts, mine, left, right):
    _, rows, width = left.shape
    return pl.pallas_call(
        first_kernel,
        out_shape=jax.ShapeDtypeStruct((2, rows // 16, 9, 8, width), jnp.float32),
        in_specs=[SMEM] * 2 + [VMEM] * 3,
        out_specs=VMEM,
        compiler_params=pltpu.CompilerParams(vmem_limit_bytes=24 * 1024 * 1024),
        cost_estimate=term_cost(left),
    )(lists, counts, mine, left, right)


def second_terms(place, lists, counts, mine, other, left, right, before):
    _, rows, width = left.shape
    tiles = rows // 16
    return pl.pallas_call(
        second_kernel,
        out_shape=(
            jax.ShapeDtypeStruct((tiles, 64, width), jnp.float32),
            jax.ShapeDtypeStruct((tiles, 64, width), jnp.bfloat16),
        ),
        in_specs=[SMEM] * 3 + [VMEM] * 5,
        out_specs=(VMEM, VMEM),
        scratch_shapes=[
            pltpu.VMEM((4 * rows, width), jnp.bfloat16),
            pltpu.VMEM((2, tiles, 9, 8, width), jnp.float32),
        ],
        compiler_params=pltpu.CompilerParams(vmem_limit_bytes=24 * 1024 * 1024),
        cost_estimate=term_cost(left),
    )(place, lists, counts, mine, other, left, right, before)


def fetch(value, shifts):
    moves = [
        (core * 8 + layer, core * 8 + (layer + shift) % 8)
        for core, shift in enumerate(shifts)
        for layer in range(8)
    ]
    return lax.ppermute(value, ("c", "z"), moves)


def body(wavefunction, block_rows, left_terms, right_terms, block_pairs, live_counts):
    _, rows, width = wavefunction.shape
    core = lax.axis_index("c").astype(jnp.int32)
    layer = lax.axis_index("z").astype(jnp.int32)
    place = jnp.stack([core, layer])
    half = rows // 2
    row_index = lax.broadcasted_iota(jnp.int32, (rows, 1), 0)
    own = jnp.where(row_index < block_rows[0], wavefunction[0], jnp.zeros_like(wavefunction[0]))
    own_half = jnp.where(core == 0, own[:half], own[half:])
    fetched = [fetch(own, (shift, -shift)) for shift in (3, 2, 1)]
    far = fetch(own_half, (4, 4))
    lists, counts, left_terms, right_terms = prepare(
        place, live_counts, block_pairs.T, left_terms, right_terms
    )
    fetched, far, lists, counts, left_terms, right_terms = lax.optimization_barrier(
        (fetched, far, lists, counts, left_terms, right_terms)
    )
    mine = jnp.concatenate([own, *fetched, far], 0)
    other = lax.ppermute(mine, "c", SWAP)
    before = first_terms(lists, counts, mine, left_terms, right_terms)
    keep, send = second_terms(
        place, lists, counts, mine, other, left_terms, right_terms, before
    )
    received = lax.ppermute(send, "c", SWAP)
    pair_sum = keep + received.astype(jnp.float32)
    pieces = lax.all_to_all(pair_sum.astype(jnp.bfloat16), LAYER, 0, 0)
    layer_sum = pieces.astype(jnp.float32).sum(0).reshape(8, 8, width)
    sigma = lax.all_to_all(layer_sum, "z", 0, 0).sum(0)
    own_tile = lax.axis_index(("y", "x", "c"))
    own_rows = own_tile * 8 + lax.broadcasted_iota(jnp.int32, (8, 1), 0)
    return jnp.where(own_rows < block_rows[0], sigma, jnp.zeros_like(sigma))[None]


def solution(mesh):
    devices = mesh.devices.reshape(4, 4, 2, mesh.shape["grp"])
    grid = Mesh(devices, ("y", "x", "c", "z"))
    everywhere = ("y", "x", "c", "z")
    placed = (
        P("z", None, None),
        P("z"),
        P(everywhere, None, None),
        P(everywhere, None, None),
        P(everywhere, None),
        P(everywhere),
    )
    return jax.shard_map(
        body, mesh=grid, in_specs=placed, out_specs=P("z", ("y", "x", "c"), None), check_vma=False
    )
```

time: 73.8 us -> 64.3 us (0.87); the launches traced: 72.8 us -> 64.2 us
  blocking collectives: 44.8 us -> 17.4 us
  starting transfers between devices: 3.44 us -> 20 us
  local copies, waits for them, and re-layouts: 6.37 us -> 0.72 us
  Pallas kernels: 3.72 us -> 9.18 us
  waiting for transfers between devices: 10.6 us -> 13 us
    all_to_all x1 -> x0, blocking collectives: 25.8 us -> none  [body(): lax.all_to_all(jnp.broadcast_to(masked, (blocks, half, width)), 'z', 0, 0)]
    ppermute x0 -> x4, starting transfers between devices: none -> 9.93 us  [fetch(): return lax.ppermute(value, ('c', 'z'), moves)]
    unnamed x5, local copies, waits for them, and re-layouts: 6.34 us -> 0.71 us
    pallas_call x1 -> x3, Pallas kernels: 3.72 us -> 9.18 us  [the longest x1 5.91 us: prepare(): pl.pallas_call(prepare_kernel, out_shape=(jax.ShapeDtypeStruct((2, 3, slo...]
    ppermute x1, starting transfers between devices: 0.09 us -> 4.1 us  [body(): received = lax.ppermute(send, 'c', SWAP)]
    ppermute x0 -> x4, waiting for transfers between devices: none -> 2.64 us  [fetch(): return lax.ppermute(value, ('c', 'z'), moves)]
    all_to_all x1, starting transfers between devices: 3.35 us -> 5.83 us  [body(): sigma = lax.all_to_all(layer_sum, 'z', 0, 0).sum(0)]
    all_to_all x1, blocking collectives: 19 us -> 17.4 us  [body(): pieces = lax.all_to_all(pair_sum.astype(jnp.bfloat16), LAYER, 0, 0)]
  transfers between devices with their start and end apart: 3 -> 7, of which waited for: 3 -> 5; matrix products, arithmetic and copies ran while one was open for 1% -> 0% of each run, Pallas kernels for 0% -> 12%
where the time goes in v2:
time: 64.3 us; the launch traced here: 64.2 us
  starting transfers between devices  20 us (31%)
  blocking collectives  17.4 us (27%)
  waiting for transfers between devices  13 us (20%)
  Pallas kernels  9.18 us (14%)
  other arithmetic  2.66 us (4%)
  between operations  1.4 us (2%)
  local copies, waits for them, and re-layouts  0.72 us (1%)
    all_to_all x1, blocking collectives, body(): pieces = lax.all_to_all(pair_sum.astype(jnp.bfloat16), LAYER, 0, 0)  17.4 us
    ppermute x4, starting transfers between devices, fetch(): return lax.ppermute(value, ('c', 'z'), moves)  9.93 us
    all_to_all x1, waiting for transfers between devices, body(): sigma = lax.all_to_all(layer_sum, 'z', 0, 0).sum(0)  8.37 us
    pallas_call x1, Pallas kernels, prepare(): pl.pallas_call(prepare_kernel, out_shape=(jax.ShapeDtypeStruct((2, 3, slo...  5.91 us
    all_to_all x1, starting transfers between devices, body(): sigma = lax.all_to_all(layer_sum, 'z', 0, 0).sum(0)  5.83 us
    ppermute x1, starting transfers between devices, body(): received = lax.ppermute(send, 'c', SWAP)  4.1 us
    ppermute x4, waiting for transfers between devices, fetch(): return lax.ppermute(value, ('c', 'z'), moves)  2.64 us
    pallas_call x1, Pallas kernels, second_terms(): pl.pallas_call(second_kernel, out_shape=(jax.ShapeDtypeStruct((tiles, 64,...  1.71 us
  transfers between devices with their start and end apart: 7, of which 5 were waited for; matrix products, arithmetic and copies ran while one was open for 0% of the time, Pallas kernels for 12%

profile of v2, /device:TPU:2, one launch (start us, length us, event | category | flops | bytes accessed | tf_op | source)
XLA Modules:
  0.0 64.2 jit_solution(8307653186903639172)
XLA Ops:
  0.7 1.0 %constant_dynamic-update-slice_fusion.4 = (bf16[1152,256]{1,0:T(8,128)(2,1)S(1)}, bf16[256,256]{1,0:T(8,128)(2,1)S(1)}) fusion(bf16[1,256,256]{2,1,0:T(8,128)(2,1)} %param.6, pred[256]{0:T(512)(128)(4,1)S(1)} %iota_compare_fusion), kind=kLoop, calls=%fused_computation.8 | loop fusion | flops 65535 | bytes 393472
  1.7 2.0 %collective-permute-start.2 = (bf16[256,256]{1,0:T(8,128)(2,1)S(1)}, bf16[256,256]{1,0:T(8,128)(2,1)S(1)}, u32[]{:S(2)}, u32[]{:S(2)}) collective-permute-start(bf16[256,256]{1,0:T(8,128)(2,1)S(1)} %get-tuple-element.34), channel_id=1, source_target_pairs={{0,1},{1,2},{2,3},{3,4},{4,5},{5,6},{6,7},{7,0},{8,15},{9,8},{10,9... | collective-permute-start | bytes 393224 | tf_op jit(solution)/shard_map/ppermute | solution.py:172
  3.7 3.3 %collective-permute-start.1 = (bf16[256,256]{1,0:T(8,128)(2,1)S(1)}, bf16[256,256]{1,0:T(8,128)(2,1)S(1)}, u32[]{:S(2)}, u32[]{:S(2)}) collective-permute-start(bf16[256,256]{1,0:T(8,128)(2,1)S(1)} %get-tuple-element.34), channel_id=1, source_target_pairs={{0,2},{1,3},{2,4},{3,5},{4,6},{5,7},{6,0},{7,1},{8,14},{9,15},{10,... | collective-permute-start | bytes 393224 | tf_op jit(solution)/shard_map/ppermute | solution.py:172
  6.9 4.0 %collective-permute-start = (bf16[256,256]{1,0:T(8,128)(2,1)S(1)}, bf16[256,256]{1,0:T(8,128)(2,1)S(1)}, u32[]{:S(2)}, u32[]{:S(2)}) collective-permute-start(bf16[256,256]{1,0:T(8,128)(2,1)S(1)} %get-tuple-element.34), channel_id=1, source_target_pairs={{0,3},{1,4},{2,5},{3,6},{4,7},{5,0},{6,1},{7,2},{8,13},{9,14},{10,... | collective-permute-start | bytes 393224 | tf_op jit(solution)/shard_map/ppermute | solution.py:172
  11.0 0.6 collective-permute-start.3
  12.3 0.1 pad_add_fusion.place_ref
  12.4 0.7 %copy-done = s32[48,2]{0,1:T(2,128)S(1)} copy-done((s32[48,2]{0,1:T(2,128)S(1)}, s32[48,2]{0,1:T(2,128)}, u32[]{:S(2)}) %copy-start) | copy-done | bytes 408
  13.0 5.9 %shard_map.64 = (s32[2,3,56]{2,1,0:T(4,128)S(1)}, s32[2]{0:T(128)S(1)}, bf16[48,256,256]{2,1,0:T(8,128)(2,1)S(1)}, bf16[48,256,256]{2,1,0:T(8,128)(2,1)S(1)}) custom-call(s32[2]{0:T(128)S(1)} %pad_add_fusion.place_ref, s32[1]{0:T(128)S(6)} %copy.12.live_ref, s32[2,48]{1,0:T(2,128)S(1)} %bitcast.12, bf16[48,256,256]{2,1,0:T(8,128)(2,1)} %left_ref.1, ...), custom_call_target="tpu_custom_call" | custom-call | bytes 25165824 | tf_op jit(solution)/shard_map/pallas_call | solution.py:63
  19.0 1.9 %collective-permute-done.3 = bf16[128,256]{1,0:T(8,128)(2,1)S(1)} collective-permute-done((bf16[128,256]{1,0:T(8,128)(2,1)S(1)}, bf16[128,256]{1,0:T(8,128)(2,1)S(1)}, u32[]{:S(2)}, u32[]{:S(2)}) %collective-permute-start.3) | collective-permute-done | bytes 65568 | tf_op jit(solution)/shard_map/ppermute | solution.py:172
  20.8 0.0 collective-permute-done.2
  20.8 0.0 collective-permute-done.1
  20.9 0.7 %collective-permute-done = bf16[256,256]{1,0:T(8,128)(2,1)S(1)} collective-permute-done((bf16[256,256]{1,0:T(8,128)(2,1)S(1)}, bf16[256,256]{1,0:T(8,128)(2,1)S(1)}, u32[]{:S(2)}, u32[]{:S(2)}) %collective-permute-start) | collective-permute-done | bytes 131104 | tf_op jit(solution)/shard_map/ppermute | solution.py:172
  21.7 0.1 collective-permute-start.4
  21.8 1.6 %shard_map.65.before = f32[2,16,9,8,256]{4,3,2,1,0:T(8,128)S(1)} custom-call(s32[2,3,56]{2,1,0:T(4,128)S(1)} %get-tuple-element.23.lists_ref, s32[2]{0:T(128)S(1)} %get-tuple-element.24.counts_ref, bf16[1152,256]{1,0:T(8,128)(2,1)S(1)} %constant_dynamic-update-slice_fusion.mine, bf16[48,256,256]{2,1,0:T(8,128)(2,1)S(1)} %get-tuple-element.29.left, ...), custom_call_target="tpu_custom_call" | custom-call | flops 1610612736 | bytes 6291456 | tf_op jit(solution)/shard_map/pallas_call | solution.py:136
  23.3 0.4 collective-permute-done.4.other
  23.7 1.7 %shard_map.66 = (f32[16,64,256]{2,1,0:T(8,128)S(1)}, bf16[16,64,256]{2,1,0:T(8,128)(2,1)S(1)}) custom-call(s32[2]{0:T(128)S(1)} %pad_add_fusion.place_ref, s32[2,3,56]{2,1,0:T(4,128)S(1)} %get-tuple-element.23.lists_ref, s32[2]{0:T(128)S(1)} %get-tuple-element.24.counts_ref, bf16[1152,256]{1,0:T(8,128)(2,1)S(1)} %constant_dynamic-update-slice_fusion.mine, ...), custom_call_target="tpu_custom_call" | custom-call | flops 1610612736 | bytes 6291456 | tf_op jit(solution)/shard_map/pallas_call | solution.py:149
  25.5 4.1 %collective-permute-start.5 = (bf16[16,64,256]{2,1,0:T(8,128)(2,1)S(1)}, bf16[16,64,256]{2,1,0:T(8,128)(2,1)S(1)}, u32[]{:S(2)}, u32[]{:S(2)}) collective-permute-start(bf16[16,64,256]{2,1,0:T(8,128)(2,1)S(1)} %get-tuple-element.32), channel_id=1, source_target_pairs={{0,8},{8,0},{1,9},{9,1},{2,10},{10,2},{3,11},{11,3},{4,12},{12,4},... | collective-permute-start | bytes 1572872 | tf_op jit(solution)/shard_map/ppermute | solution.py:198
  29.6 1.5 %collective-permute-done.5 = bf16[16,64,256]{2,1,0:T(8,128)(2,1)S(1)} collective-permute-done((bf16[16,64,256]{2,1,0:T(8,128)(2,1)S(1)}, bf16[16,64,256]{2,1,0:T(8,128)(2,1)S(1)}, u32[]{:S(2)}, u32[]{:S(2)}) %collective-permute-start.5) | collective-permute-done | bytes 524320 | tf_op jit(solution)/shard_map/ppermute | solution.py:198
  31.1 0.2 add_convert_fusion
  31.3 17.4 %all_to_all.10 = bf16[16,64,256]{2,1,0:T(8,128)(2,1)S(1)} all-to-all(bf16[16,64,256]{2,1,0:T(8,128)(2,1)S(1)} %add_convert_fusion), channel_id=1, replica_groups=mesh['y'=4,'x'=4,'c'=2,'z'=8] {'y','x'}, dimensions={0} | all-to-all | bytes 1048576 | tf_op jit(solution)/shard_map/all_to_all | solution.py:200
  48.6 0.7 %convert_reduce_fusion = f32[64,256]{1,0:T(8,128)} fusion(bf16[16,64,256]{2,1,0:T(8,128)(2,1)S(1)} %all_to_all.10), kind=kLoop, calls=%fused_computation | loop fusion | flops 507904 | bytes 589824 | tf_op jit(solution)/shard_map/reduce_sum | solution.py:201
  49.3 5.8 %all-to-all-start.1 = ((f32[8,8,256]{2,1,0:T(8,128)}), f32[8,8,256]{2,1,0:T(8,128)S(1)}, u32[]{:S(2)}, u32[]{:S(2)}) async-start(f32[8,8,256]{2,1,0:T(8,128)} %bitcast.5), calls=%async_computation.1 | async-start | bytes 131072 | tf_op jit(solution)/shard_map/all_to_all | solution.py:202
  55.2 8.4 %all-to-all-done.1 = f32[8,8,256]{2,1,0:T(8,128)S(1)} async-done(((f32[8,8,256]{2,1,0:T(8,128)}), f32[8,8,256]{2,1,0:T(8,128)S(1)}, u32[]{:S(2)}, u32[]{:S(2)}) %all-to-all-start.1) | async-done | bytes 65568 | tf_op jit(solution)/shard_map/all_to_all | solution.py:202
  63.6 0.7 %bitcast_select_fusion.1 = f32[1,8,256]{2,1,0:T(8,128)} fusion(f32[8,256]{1,0:T(8,128)S(1)} %reduce_sum.21, pred[8]{0:T(512)(128)(4,1)S(1)} %add_compare_fusion), kind=kLoop, calls=%fused_computation.9 | loop fusion | flops 2048 | bytes 16392 | tf_op jit(solution)/shard_map/jit(_where)/select_n | solution.py:205
  (9 shorter events, 0.1 us)
Async XLA Ops:
  1.7 19.2 %collective-permute-start.2 = (bf16[256,256]{1,0:T(8,128)(2,1)S(1)}, bf16[256,256]{1,0:T(8,128)(2,1)S(1)}, u32[]{:S(2)}, u32[]{:S(2)}) collective-permute-start(bf16[256,256]{1,0:T(8,128)(2,1)S(1)} %get-tuple-element.34), channel_id=1, source_target_pairs={{0,1},{1,2},{2,3},{3,4},{4,5},{5,6},{6,7},{7,0},{8,15},{9,8},{10,9... | collective-permute-start | bytes 393224 | tf_op jit(solution)/shard_map/ppermute | solution.py:172
  3.7 17.2 %collective-permute-start.1 = (bf16[256,256]{1,0:T(8,128)(2,1)S(1)}, bf16[256,256]{1,0:T(8,128)(2,1)S(1)}, u32[]{:S(2)}, u32[]{:S(2)}) collective-permute-start(bf16[256,256]{1,0:T(8,128)(2,1)S(1)} %get-tuple-element.34), channel_id=1, source_target_pairs={{0,2},{1,3},{2,4},{3,5},{4,6},{5,7},{6,0},{7,1},{8,14},{9,15},{10,... | collective-permute-start | bytes 393224 | tf_op jit(solution)/shard_map/ppermute | solution.py:172
  6.9 14.6 %collective-permute-start = (bf16[256,256]{1,0:T(8,128)(2,1)S(1)}, bf16[256,256]{1,0:T(8,128)(2,1)S(1)}, u32[]{:S(2)}, u32[]{:S(2)}) collective-permute-start(bf16[256,256]{1,0:T(8,128)(2,1)S(1)} %get-tuple-element.34), channel_id=1, source_target_pairs={{0,3},{1,4},{2,5},{3,6},{4,7},{5,0},{6,1},{7,2},{8,13},{9,14},{10,... | collective-permute-start | bytes 393224 | tf_op jit(solution)/shard_map/ppermute | solution.py:172
  11.0 9.8 %collective-permute-start.3 = (bf16[128,256]{1,0:T(8,128)(2,1)S(1)}, bf16[128,256]{1,0:T(8,128)(2,1)S(1)}, u32[]{:S(2)}, u32[]{:S(2)}) collective-permute-start(bf16[128,256]{1,0:T(8,128)(2,1)S(1)} %slice_select_fusion), channel_id=1, source_target_pairs={{0,4},{1,5},{2,6},{3,7},{4,0},{5,1},{6,2},{7,3},{8,12},{9,13},{10,... | collective-permute-start | bytes 196616 | tf_op jit(solution)/shard_map/ppermute | solution.py:172
  12.4 0.7 %copy-start = (s32[48,2]{0,1:T(2,128)S(1)}, s32[48,2]{0,1:T(2,128)}, u32[]{:S(2)}) copy-start(s32[48,2]{0,1:T(2,128)} %param.10) | copy-start | bytes 1156
  21.7 2.1 %collective-permute-start.4 = (bf16[1152,256]{1,0:T(8,128)(2,1)S(1)}, bf16[1152,256]{1,0:T(8,128)(2,1)S(1)}, u32[]{:S(2)}, u32[]{:S(2)}) collective-permute-start(bf16[1152,256]{1,0:T(8,128)(2,1)S(1)} %constant_dynamic-update-slice_fusion.mine), channel_id=1, source_target_pairs={{0,8},{8,0},{1,9},{9,1},{2,10},{10,2},{3,11},{11,3},{4,12},{12,4},... | collective-permute-start | bytes 1769480 | tf_op jit(solution)/shard_map/ppermute | solution.py:193
  25.5 5.6 %collective-permute-start.5 = (bf16[16,64,256]{2,1,0:T(8,128)(2,1)S(1)}, bf16[16,64,256]{2,1,0:T(8,128)(2,1)S(1)}, u32[]{:S(2)}, u32[]{:S(2)}) collective-permute-start(bf16[16,64,256]{2,1,0:T(8,128)(2,1)S(1)} %get-tuple-element.32), channel_id=1, source_target_pairs={{0,8},{8,0},{1,9},{9,1},{2,10},{10,2},{3,11},{11,3},{4,12},{12,4},... | collective-permute-start | bytes 1572872 | tf_op jit(solution)/shard_map/ppermute | solution.py:198
  49.3 14.2 %all-to-all-start.1 = ((f32[8,8,256]{2,1,0:T(8,128)}), f32[8,8,256]{2,1,0:T(8,128)S(1)}, u32[]{:S(2)}, u32[]{:S(2)}) async-start(f32[8,8,256]{2,1,0:T(8,128)} %bitcast.5), calls=%async_computation.1 | async-start | bytes 131072 | tf_op jit(solution)/shard_map/all_to_all | solution.py:202

commit v3 on v2

v3 whole, which is shorter than its diff:
```python
import jax
import jax.numpy as jnp
from jax import lax
from jax.experimental import pallas as pl
from jax.experimental.pallas import tpu as pltpu
from jax.sharding import Mesh, PartitionSpec as P

GROUP = 8
PARTS = 6
LAYER = ("y", "x")
SWAP = [(0, 1), (1, 0)]
SMEM = pl.BlockSpec(memory_space=pltpu.SMEM)
VMEM = pl.BlockSpec(memory_space=pltpu.VMEM)


def add_group(lists_ref, which, at, size, psi, left, right, acc):
    tiles, width = acc.shape[1], acc.shape[-1]
    products = []
    for i in range(size):
        slot, source = lists_ref[which, 0, at + i], lists_ref[which, 1, at + i]
        block = psi[pl.ds(pl.multiple_of(source * width, width), width)]
        product = jnp.dot(left[slot], block, preferred_element_type=jnp.float32)
        products.append(product.astype(jnp.bfloat16))
    for i in range(size):
        slot, target = lists_ref[which, 0, at + i], lists_ref[which, 2, at + i]
        term = jnp.dot(products[i], right[slot], preferred_element_type=jnp.float32)
        term = term.reshape(tiles, 2, 8, width)
        for c in range(2):
            acc[c, :, target] += term[:, c]


def add_terms(which, lists_ref, counts_ref, psi, left, right, acc, ready=None):
    count = counts_ref[which]
    groups = (count + GROUP // 2 - 1) // GROUP

    def step(j, carry):
        if ready is not None:
            ready(j * GROUP, GROUP)
        add_group(lists_ref, which, j * GROUP, GROUP, psi, left, right, acc)
        return carry

    lax.fori_loop(0, groups, step, 0)

    @pl.when(count > groups * GROUP)
    def _():
        if ready is not None:
            ready(groups * GROUP, GROUP // 2)
        add_group(lists_ref, which, groups * GROUP, GROUP // 2, psi, left, right, acc)


def prepare_kernel(
    place_ref, live_ref, pairs_ref, own, left_ref, right_ref,
    lists_ref, counts_ref, left_here, right_here, acc, waited, left_sem, right_sem,
):
    part = left_ref.shape[0] // PARTS

    def loads(i):
        slots = pl.ds(i * part, part)
        return (
            pltpu.make_async_copy(left_ref.at[slots], left_here.at[slots], left_sem.at[i]),
            pltpu.make_async_copy(right_ref.at[slots], right_here.at[slots], right_sem.at[i]),
        )

    for i in range(PARTS):
        for load in loads(i):
            load.start()
    acc[...] = jnp.zeros_like(acc)
    core, layer = place_ref[0], place_ref[1]

    def clear(i, carry):
        for which in range(3):
            lists_ref[which, 0, i] = 0
            lists_ref[which, 1, i] = 0
            lists_ref[which, 2, i] = 8
        return carry

    lax.fori_loop(0, lists_ref.shape[2], clear, 0)
    for which in range(3):
        counts_ref[which] = 0

    def put(k, carry):
        ahead = (pairs_ref[0, k] - layer) & 7
        hops = jnp.minimum(ahead, 8 - ahead)
        theirs = 1 - ((ahead > 4).astype(jnp.int32) ^ core)
        which = jnp.where(hops == 0, 0, jnp.where(hops == 4, 2, 1 + theirs))
        source = jnp.where(hops == 0, 0, 4 - hops)
        at = counts_ref[which]
        lists_ref[which, 0, at] = k
        lists_ref[which, 1, at] = source
        lists_ref[which, 2, at] = pairs_ref[1, k]
        counts_ref[which] = at + 1
        return carry

    lax.fori_loop(0, live_ref[0], put, 0)
    waited[0] = 0

    def ready(at, size):
        last = lists_ref[0, 0, at]
        for i in range(1, size):
            last = jnp.maximum(last, lists_ref[0, 0, at + i])
        until = last // part + 1
        for i in range(PARTS):

            @pl.when((i >= waited[0]) & (i < until))
            def _():
                for load in loads(i):
                    load.wait()

        waited[0] = jnp.maximum(waited[0], until)

    add_terms(0, lists_ref, counts_ref, own, left_here, right_here, acc, ready)
    for i in range(PARTS):

        @pl.when(i >= waited[0])
        def _():
            for load in loads(i):
                load.wait()


def prepare(place, live, pairs, own, left, right):
    slots, rows, width = left.shape
    return pl.pallas_call(
        prepare_kernel,
        out_shape=(
            jax.ShapeDtypeStruct((3, 3, slots + GROUP), jnp.int32),
            jax.ShapeDtypeStruct((3,), jnp.int32),
            jax.ShapeDtypeStruct(left.shape, left.dtype),
            jax.ShapeDtypeStruct(right.shape, right.dtype),
            jax.ShapeDtypeStruct((2, rows // 16, 9, 8, width), jnp.float32),
        ),
        in_specs=[SMEM] * 3 + [VMEM] + [pl.BlockSpec(memory_space=pl.ANY)] * 2,
        out_specs=(SMEM, SMEM, VMEM, VMEM, VMEM),
        scratch_shapes=[
            pltpu.SMEM((1,), jnp.int32),
            pltpu.SemaphoreType.DMA((PARTS,)),
            pltpu.SemaphoreType.DMA((PARTS,)),
        ],
        compiler_params=pltpu.CompilerParams(vmem_limit_bytes=37 * 1024 * 1024),
        cost_estimate=pl.CostEstimate(
            flops=0, bytes_accessed=4 * (left.size + right.size), transcendentals=0
        ),
    )(place, live, pairs, own, left, right)


def middle_terms(which, lists, counts, blocks, left, right, before):
    def kernel(lists_ref, counts_ref, psi, left, right, before_ref, acc):
        add_terms(which, lists_ref, counts_ref, psi, left, right, acc)

    return pl.pallas_call(
        kernel,
        out_shape=jax.ShapeDtypeStruct(before.shape, before.dtype),
        in_specs=[SMEM] * 2 + [VMEM] * 4,
        out_specs=VMEM,
        input_output_aliases={5: 0},
        compiler_params=pltpu.CompilerParams(vmem_limit_bytes=16 * 1024 * 1024),
        cost_estimate=term_cost(left),
    )(lists, counts, blocks, left, right, before)


def last_kernel(
    place_ref, lists_ref, counts_ref, mine, other, left, right, before, keep_ref, send_ref, psi, acc
):
    core = place_ref[0]
    tiles, share, width = send_ref.shape
    half = width // 2
    own_rows = pl.ds(pl.multiple_of(core * half, half), half)
    their_rows = pl.ds(pl.multiple_of((1 - core) * half, half), half)
    psi[own_rows] = mine[:half]
    psi[their_rows] = other[:half]
    psi[width:] = other[width:]
    acc[...] = before[...]
    add_terms(2, lists_ref, counts_ref, psi, left, right, acc)
    for tile in range(tiles):
        keep_ref[tile] = acc[core, tile, :8].reshape(share, width)
        send_ref[tile] = acc[1 - core, tile, :8].reshape(share, width).astype(send_ref.dtype)


def term_cost(left):
    slots, rows, width = left.shape
    return pl.CostEstimate(
        flops=2 * rows * rows * width * slots,
        bytes_accessed=2 * rows * width * slots,
        transcendentals=0,
    )


def last_terms(place, lists, counts, mine, other, left, right, before):
    _, rows, width = left.shape
    tiles = rows // 16
    return pl.pallas_call(
        last_kernel,
        out_shape=(
            jax.ShapeDtypeStruct((tiles, 64, width), jnp.float32),
            jax.ShapeDtypeStruct((tiles, 64, width), jnp.bfloat16),
        ),
        in_specs=[SMEM] * 3 + [VMEM] * 5,
        out_specs=(VMEM, VMEM),
        scratch_shapes=[
            pltpu.VMEM((4 * rows, width), jnp.bfloat16),
            pltpu.VMEM((2, tiles, 9, 8, width), jnp.float32),
        ],
        compiler_params=pltpu.CompilerParams(vmem_limit_bytes=16 * 1024 * 1024),
        cost_estimate=term_cost(left),
    )(place, lists, counts, mine, other, left, right, before)


def fetch(value, shifts):
    moves = [
        (core * 8 + layer, core * 8 + (layer + shift) % 8)
        for core, shift in enumerate(shifts)
        for layer in range(8)
    ]
    return lax.ppermute(value, ("c", "z"), moves)


def body(wavefunction, block_rows, left_terms, right_terms, block_pairs, live_counts):
    _, rows, width = wavefunction.shape
    core = lax.axis_index("c").astype(jnp.int32)
    layer = lax.axis_index("z").astype(jnp.int32)
    place = jnp.stack([core, layer])
    half = rows // 2
    row_index = lax.broadcasted_iota(jnp.int32, (rows, 1), 0)
    own = jnp.where(row_index < block_rows[0], wavefunction[0], jnp.zeros_like(wavefunction[0]))
    own_half = jnp.where(core == 0, own[:half], own[half:])
    fetched = [fetch(own, (shift, -shift)) for shift in (3, 2, 1)]
    far = fetch(own_half, (4, 4))
    prepared = prepare(place, live_counts, block_pairs.T, own, left_terms, right_terms)
    fetched, far, prepared = lax.optimization_barrier((fetched, far, prepared))
    lists, counts, left, right, sums = prepared
    mine = jnp.concatenate([far, far, *fetched], 0)
    other = lax.ppermute(mine, "c", SWAP)
    sums = middle_terms(1, lists, counts, mine, left, right, sums)
    keep, send = last_terms(place, lists, counts, mine, other, left, right, sums)
    received = lax.ppermute(send, "c", SWAP)
    pair_sum = keep + received.astype(jnp.float32)
    pieces = lax.all_to_all(pair_sum.astype(jnp.bfloat16), LAYER, 0, 0)
    layer_sum = pieces.astype(jnp.float32).sum(0).reshape(8, 8, width)
    sigma = lax.all_to_all(layer_sum, "z", 0, 0).sum(0)
    own_tile = lax.axis_index(("y", "x", "c"))
    own_rows = own_tile * 8 + lax.broadcasted_iota(jnp.int32, (8, 1), 0)
    return jnp.where(own_rows < block_rows[0], sigma, jnp.zeros_like(sigma))[None]


def solution(mesh):
    devices = mesh.devices.reshape(4, 4, 2, mesh.shape["grp"])
    grid = Mesh(devices, ("y", "x", "c", "z"))
    everywhere = ("y", "x", "c", "z")
    placed = (
        P("z", None, None),
        P("z"),
        P(everywhere, None, None),
        P(everywhere, None, None),
        P(everywhere, None),
        P(everywhere),
    )
    return jax.shard_map(
        body, mesh=grid, in_specs=placed, out_specs=P("z", ("y", "x", "c"), None), check_vma=False
    )
```

time: 64.3 us -> 62.8 us (0.977); the launches traced: 64.2 us -> 62 us
  starting transfers between devices: 20 us -> 13.9 us
  blocking collectives: 17.4 us -> 20.9 us
    ppermute x1, starting transfers between devices: 4.1 us -> 0.09 us  [body(): received = lax.ppermute(send, 'c', SWAP)]
    all_to_all x1, blocking collectives: 17.4 us -> 20.9 us  [body(): pieces = lax.all_to_all(pair_sum.astype(jnp.bfloat16), LAYER, 0, 0)]
    all_to_all x1, starting transfers between devices: 5.83 us -> 3.82 us  [body(): sigma = lax.all_to_all(layer_sum, 'z', 0, 0).sum(0)]
    select_n x0 -> x1, other arithmetic: none -> 1.01 us  [body(): jnp.where(row_index < block_rows[0], wavefunction[0], jnp.zeros_like(wave...]
    unnamed x1 -> x0, other arithmetic: 1.01 us -> none
  transfers between devices with their start and end apart: 7 -> 7, of which waited for: 5 -> 5; matrix products, arithmetic and copies ran while one was open for 0% -> 0% of each run, Pallas kernels for 12% -> 11%
where the time goes in v3:
time: 62.8 us; the launch traced here: 62 us
  blocking collectives  20.9 us (33%)
  starting transfers between devices  13.9 us (22%)
  waiting for transfers between devices  13.6 us (22%)
  Pallas kernels  8.83 us (14%)
  other arithmetic  2.61 us (4%)
  between operations  1.41 us (2%)
  local copies, waits for them, and re-layouts  0.72 us (1%)
    all_to_all x1, blocking collectives, body(): pieces = lax.all_to_all(pair_sum.astype(jnp.bfloat16), LAYER, 0, 0)  20.9 us
    ppermute x4, starting transfers between devices, fetch(): return lax.ppermute(value, ('c', 'z'), moves)  9.93 us
    all_to_all x1, waiting for transfers between devices, body(): sigma = lax.all_to_all(layer_sum, 'z', 0, 0).sum(0)  8.37 us
    pallas_call x1, Pallas kernels, prepare(): pl.pallas_call(prepare_kernel, out_shape=(jax.ShapeDtypeStruct((3, 3, slo...  5.95 us
    all_to_all x1, starting transfers between devices, body(): sigma = lax.all_to_all(layer_sum, 'z', 0, 0).sum(0)  3.82 us
    ppermute x4, waiting for transfers between devices, fetch(): return lax.ppermute(value, ('c', 'z'), moves)  2.6 us
    ppermute x1, waiting for transfers between devices, body(): received = lax.ppermute(send, 'c', SWAP)  1.9 us
    pallas_call x1, Pallas kernels, last_terms(): pl.pallas_call(last_kernel, out_shape=(jax.ShapeDtypeStruct((tiles, 64, w...  1.76 us
  transfers between devices with their start and end apart: 7, of which 5 were waited for; matrix products, arithmetic and copies ran while one was open for 0% of the time, Pallas kernels for 11%

profile of v3, /device:TPU:2, one launch (start us, length us, event | category | flops | bytes accessed | tf_op | source)
XLA Modules:
  0.0 62.0 jit_solution(8117634982173733210)
XLA Ops:
  0.7 1.0 %bitcast_select_fusion.own = bf16[256,256]{1,0:T(8,128)(2,1)S(1)} fusion(bf16[1,256,256]{2,1,0:T(8,128)(2,1)} %param.6, pred[256]{0:T(512)(128)(4,1)S(1)} %iota_compare_fusion), kind=kLoop, calls=%fused_computation.2 | loop fusion | flops 65536 | bytes 262400 | tf_op jit(solution)/shard_map/jit(_where)/select_n | solution.py:223
  1.7 2.0 %collective-permute-start.2 = (bf16[256,256]{1,0:T(8,128)(2,1)S(1)}, bf16[256,256]{1,0:T(8,128)(2,1)S(1)}, u32[]{:S(2)}, u32[]{:S(2)}) collective-permute-start(bf16[256,256]{1,0:T(8,128)(2,1)S(1)} %bitcast_select_fusion.own), channel_id=1, source_target_pairs={{0,1},{1,2},{2,3},{3,4},{4,5},{5,6},{6,7},{7,0},{8,15},{9,8},{10,9... | collective-permute-start | bytes 393224 | tf_op jit(solution)/shard_map/ppermute | solution.py:213
  3.7 3.3 %collective-permute-start.1 = (bf16[256,256]{1,0:T(8,128)(2,1)S(1)}, bf16[256,256]{1,0:T(8,128)(2,1)S(1)}, u32[]{:S(2)}, u32[]{:S(2)}) collective-permute-start(bf16[256,256]{1,0:T(8,128)(2,1)S(1)} %bitcast_select_fusion.own), channel_id=1, source_target_pairs={{0,2},{1,3},{2,4},{3,5},{4,6},{5,7},{6,0},{7,1},{8,14},{9,15},{10,... | collective-permute-start | bytes 393224 | tf_op jit(solution)/shard_map/ppermute | solution.py:213
  6.9 4.0 %collective-permute-start = (bf16[256,256]{1,0:T(8,128)(2,1)S(1)}, bf16[256,256]{1,0:T(8,128)(2,1)S(1)}, u32[]{:S(2)}, u32[]{:S(2)}) collective-permute-start(bf16[256,256]{1,0:T(8,128)(2,1)S(1)} %bitcast_select_fusion.own), channel_id=1, source_target_pairs={{0,3},{1,4},{2,5},{3,6},{4,7},{5,0},{6,1},{7,2},{8,13},{9,14},{10,... | collective-permute-start | bytes 393224 | tf_op jit(solution)/shard_map/ppermute | solution.py:213
  11.0 0.6 %collective-permute-start.3 = (bf16[128,256]{1,0:T(8,128)(2,1)S(1)}, bf16[128,256]{1,0:T(8,128)(2,1)S(1)}, u32[]{:S(2)}, u32[]{:S(2)}) collective-permute-start(bf16[128,256]{1,0:T(8,128)(2,1)S(1)} %slice_select_fusion), channel_id=1, source_target_pairs={{0,4},{1,5},{2,6},{3,7},{4,0},{5,1},{6,2},{7,3},{8,12},{9,13},{10,... | collective-permute-start | bytes 196616 | tf_op jit(solution)/shard_map/ppermute | solution.py:213
  12.3 0.1 pad_add_fusion.place_ref
  12.4 0.7 %copy-done = s32[48,2]{0,1:T(2,128)S(1)} copy-done((s32[48,2]{0,1:T(2,128)S(1)}, s32[48,2]{0,1:T(2,128)}, u32[]{:S(2)}) %copy-start) | copy-done | bytes 408
  13.0 5.9 %shard_map.64 = (s32[3,3,56]{2,1,0:T(4,128)S(1)}, s32[3]{0:T(128)S(1)}, bf16[48,256,256]{2,1,0:T(8,128)(2,1)S(1)}, bf16[48,256,256]{2,1,0:T(8,128)(2,1)S(1)}, f32[2,16,9,8,256]{4,3,2,1,0:T(8,128)S(1)}) custom-call(s32[2]{0:T(128)S(1)} %pad_add_fusion.place_ref, s32[1]{0:T(128)S(6)} %copy.14.live_ref, s32[2,48]{1,0:T(2,128)S(1)} %bitcast.11, ...), custom_call_target="tpu_custom_call" | custom-call | bytes 25165824 | tf_op jit(solution)/shard_map/pallas_call | solution.py:122
  19.0 1.9 %collective-permute-done.3 = bf16[128,256]{1,0:T(8,128)(2,1)S(1)} collective-permute-done((bf16[128,256]{1,0:T(8,128)(2,1)S(1)}, bf16[128,256]{1,0:T(8,128)(2,1)S(1)}, u32[]{:S(2)}, u32[]{:S(2)}) %collective-permute-start.3) | collective-permute-done | bytes 65568 | tf_op jit(solution)/shard_map/ppermute | solution.py:213
  20.8 0.0 collective-permute-done.2
  20.8 0.0 collective-permute-done.1
  20.9 0.7 %collective-permute-done = bf16[256,256]{1,0:T(8,128)(2,1)S(1)} collective-permute-done((bf16[256,256]{1,0:T(8,128)(2,1)S(1)}, bf16[256,256]{1,0:T(8,128)(2,1)S(1)}, u32[]{:S(2)}, u32[]{:S(2)}) %collective-permute-start) | collective-permute-done | bytes 131104 | tf_op jit(solution)/shard_map/ppermute | solution.py:213
  21.7 0.1 collective-permute-start.4
  21.8 1.1 %shard_map.65.before = f32[2,16,9,8,256]{4,3,2,1,0:T(8,128)S(1)} custom-call(s32[3,3,56]{2,1,0:T(4,128)S(1)} %get-tuple-element.26.lists_ref, s32[3]{0:T(128)S(1)} %get-tuple-element.27.counts_ref, bf16[1024,256]{1,0:T(8,128)(2,1)S(1)} %constant_dynamic-update-slice_fusion.psi.mine, ...), custom_call_target="tpu_custom_call", output_to_operand_aliasing={{}: (5, {})} | custom-call | flops 1610612736 | bytes 6291456 | tf_op jit(solution)/shard_map/pallas_call | solution.py:149
  22.9 0.8 %collective-permute-done.4.other = bf16[1024,256]{1,0:T(8,128)(2,1)S(1)} collective-permute-done((bf16[1024,256]{1,0:T(8,128)(2,1)S(1)}, bf16[1024,256]{1,0:T(8,128)(2,1)S(1)}, u32[]{:S(2)}, u32[]{:S(2)}) %collective-permute-start.4) | collective-permute-done | bytes 524320 | tf_op jit(solution)/shard_map/ppermute | solution.py:231
  23.7 1.8 %shard_map.66 = (f32[16,64,256]{2,1,0:T(8,128)S(1)}, bf16[16,64,256]{2,1,0:T(8,128)(2,1)S(1)}) custom-call(s32[2]{0:T(128)S(1)} %pad_add_fusion.place_ref, s32[3,3,56]{2,1,0:T(4,128)S(1)} %get-tuple-element.26.lists_ref, s32[3]{0:T(128)S(1)} %get-tuple-element.27.counts_ref, bf16[1024,256]{1,0:T(8,128)(2,1)S(1)} %constant_dynamic-update-slice_fusion.psi.mine, ...), custom_call_target="tpu_custom_call" | custom-call | flops 1610612736 | bytes 6291456 | tf_op jit(solution)/shard_map/pallas_call | solution.py:190
  25.4 0.1 collective-permute-start.5
  25.5 1.9 %collective-permute-done.5 = bf16[16,64,256]{2,1,0:T(8,128)(2,1)S(1)} collective-permute-done((bf16[16,64,256]{2,1,0:T(8,128)(2,1)S(1)}, bf16[16,64,256]{2,1,0:T(8,128)(2,1)S(1)}, u32[]{:S(2)}, u32[]{:S(2)}) %collective-permute-start.5) | collective-permute-done | bytes 524320 | tf_op jit(solution)/shard_map/ppermute | solution.py:234
  27.4 0.1 add_convert_fusion
  27.6 20.9 %all_to_all.10 = bf16[16,64,256]{2,1,0:T(8,128)(2,1)S(1)} all-to-all(bf16[16,64,256]{2,1,0:T(8,128)(2,1)S(1)} %add_convert_fusion), channel_id=1, replica_groups=mesh['y'=4,'x'=4,'c'=2,'z'=8] {'y','x'}, dimensions={0} | all-to-all | bytes 1048576 | tf_op jit(solution)/shard_map/all_to_all | solution.py:236
  48.4 0.7 %convert_reduce_fusion = f32[64,256]{1,0:T(8,128)} fusion(bf16[16,64,256]{2,1,0:T(8,128)(2,1)S(1)} %all_to_all.10), kind=kLoop, calls=%fused_computation | loop fusion | flops 507904 | bytes 589824 | tf_op jit(solution)/shard_map/reduce_sum | solution.py:237
  49.1 3.8 %all-to-all-start.1 = ((f32[8,8,256]{2,1,0:T(8,128)}), f32[8,8,256]{2,1,0:T(8,128)S(1)}, u32[]{:S(2)}, u32[]{:S(2)}) async-start(f32[8,8,256]{2,1,0:T(8,128)} %bitcast.5), calls=%async_computation.1 | async-start | bytes 131072 | tf_op jit(solution)/shard_map/all_to_all | solution.py:238
  53.0 8.4 %all-to-all-done.1 = f32[8,8,256]{2,1,0:T(8,128)S(1)} async-done(((f32[8,8,256]{2,1,0:T(8,128)}), f32[8,8,256]{2,1,0:T(8,128)S(1)}, u32[]{:S(2)}, u32[]{:S(2)}) %all-to-all-start.1) | async-done | bytes 65568 | tf_op jit(solution)/shard_map/all_to_all | solution.py:238
  61.3 0.7 %bitcast_select_fusion.1 = f32[1,8,256]{2,1,0:T(8,128)} fusion(f32[8,256]{1,0:T(8,128)S(1)} %reduce_sum.21, pred[8]{0:T(512)(128)(4,1)S(1)} %add_compare_fusion), kind=kLoop, calls=%fused_computation.9 | loop fusion | flops 2048 | bytes 16392 | tf_op jit(solution)/shard_map/jit(_where)/select_n | solution.py:241
  (10 shorter events, 0.1 us)
Async XLA Ops:
  1.7 19.2 %collective-permute-start.2 = (bf16[256,256]{1,0:T(8,128)(2,1)S(1)}, bf16[256,256]{1,0:T(8,128)(2,1)S(1)}, u32[]{:S(2)}, u32[]{:S(2)}) collective-permute-start(bf16[256,256]{1,0:T(8,128)(2,1)S(1)} %bitcast_select_fusion.own), channel_id=1, source_target_pairs={{0,1},{1,2},{2,3},{3,4},{4,5},{5,6},{6,7},{7,0},{8,15},{9,8},{10,9... | collective-permute-start | bytes 393224 | tf_op jit(solution)/shard_map/ppermute | solution.py:213
  3.7 17.2 %collective-permute-start.1 = (bf16[256,256]{1,0:T(8,128)(2,1)S(1)}, bf16[256,256]{1,0:T(8,128)(2,1)S(1)}, u32[]{:S(2)}, u32[]{:S(2)}) collective-permute-start(bf16[256,256]{1,0:T(8,128)(2,1)S(1)} %bitcast_select_fusion.own), channel_id=1, source_target_pairs={{0,2},{1,3},{2,4},{3,5},{4,6},{5,7},{6,0},{7,1},{8,14},{9,15},{10,... | collective-permute-start | bytes 393224 | tf_op jit(solution)/shard_map/ppermute | solution.py:213
  6.9 14.6 %collective-permute-start = (bf16[256,256]{1,0:T(8,128)(2,1)S(1)}, bf16[256,256]{1,0:T(8,128)(2,1)S(1)}, u32[]{:S(2)}, u32[]{:S(2)}) collective-permute-start(bf16[256,256]{1,0:T(8,128)(2,1)S(1)} %bitcast_select_fusion.own), channel_id=1, source_target_pairs={{0,3},{1,4},{2,5},{3,6},{4,7},{5,0},{6,1},{7,2},{8,13},{9,14},{10,... | collective-permute-start | bytes 393224 | tf_op jit(solution)/shard_map/ppermute | solution.py:213
  11.0 9.8 %collective-permute-start.3 = (bf16[128,256]{1,0:T(8,128)(2,1)S(1)}, bf16[128,256]{1,0:T(8,128)(2,1)S(1)}, u32[]{:S(2)}, u32[]{:S(2)}) collective-permute-start(bf16[128,256]{1,0:T(8,128)(2,1)S(1)} %slice_select_fusion), channel_id=1, source_target_pairs={{0,4},{1,5},{2,6},{3,7},{4,0},{5,1},{6,2},{7,3},{8,12},{9,13},{10,... | collective-permute-start | bytes 196616 | tf_op jit(solution)/shard_map/ppermute | solution.py:213
  12.4 0.7 %copy-start = (s32[48,2]{0,1:T(2,128)S(1)}, s32[48,2]{0,1:T(2,128)}, u32[]{:S(2)}) copy-start(s32[48,2]{0,1:T(2,128)} %param.10) | copy-start | bytes 1156
  21.7 2.0 %collective-permute-start.4 = (bf16[1024,256]{1,0:T(8,128)(2,1)S(1)}, bf16[1024,256]{1,0:T(8,128)(2,1)S(1)}, u32[]{:S(2)}, u32[]{:S(2)}) collective-permute-start(bf16[1024,256]{1,0:T(8,128)(2,1)S(1)} %constant_dynamic-update-slice_fusion.psi.mine), channel_id=1, source_target_pairs={{0,8},{8,0},{1,9},{9,1},{2,10},{10,2},{3,11},{11,3},{4,12},{12,4},... | collective-permute-start | bytes 1572872 | tf_op jit(solution)/shard_map/ppermute | solution.py:231
  25.4 2.0 %collective-permute-start.5 = (bf16[16,64,256]{2,1,0:T(8,128)(2,1)S(1)}, bf16[16,64,256]{2,1,0:T(8,128)(2,1)S(1)}, u32[]{:S(2)}, u32[]{:S(2)}) collective-permute-start(bf16[16,64,256]{2,1,0:T(8,128)(2,1)S(1)} %get-tuple-element.36), channel_id=1, source_target_pairs={{0,8},{8,0},{1,9},{9,1},{2,10},{10,2},{3,11},{11,3},{4,12},{12,4},... | collective-permute-start | bytes 1572872 | tf_op jit(solution)/shard_map/ppermute | solution.py:234
  49.1 12.2 %all-to-all-start.1 = ((f32[8,8,256]{2,1,0:T(8,128)}), f32[8,8,256]{2,1,0:T(8,128)S(1)}, u32[]{:S(2)}, u32[]{:S(2)}) async-start(f32[8,8,256]{2,1,0:T(8,128)} %bitcast.5), calls=%async_computation.1 | async-start | bytes 131072 | tf_op jit(solution)/shard_map/all_to_all | solution.py:238

commit v4 on v3

--- a/solution.py
+++ b/solution.py
@@ -7,7 +7,6 @@
 
 GROUP = 8
 PARTS = 6
-LAYER = ("y", "x")
 SWAP = [(0, 1), (1, 0)]
 SMEM = pl.BlockSpec(memory_space=pltpu.SMEM)
 VMEM = pl.BlockSpec(memory_space=pltpu.VMEM)
@@ -232,10 +231,20 @@
     sums = middle_terms(1, lists, counts, mine, left, right, sums)
     keep, send = last_terms(place, lists, counts, mine, other, left, right, sums)
     received = lax.ppermute(send, "c", SWAP)
-    pair_sum = keep + received.astype(jnp.float32)
-    pieces = lax.all_to_all(pair_sum.astype(jnp.bfloat16), LAYER, 0, 0)
-    layer_sum = pieces.astype(jnp.float32).sum(0).reshape(8, 8, width)
-    sigma = lax.all_to_all(layer_sum, "z", 0, 0).sum(0)
+    pair_sum = (keep + received.astype(jnp.float32)).reshape(4, 256, width)
+    line = lax.axis_index("y")
+
+    def piece(shift):
+        return lax.dynamic_index_in_dim(pair_sum, (line + shift) % 4, 0, False)
+
+    line_sum = piece(0)
+    for shift in (2, 1, 3):
+        moves = [(i, (i + shift) % 4) for i in range(4)]
+        arrived = lax.ppermute(piece(shift).astype(jnp.bfloat16), "y", moves)
+        line_sum += arrived.astype(jnp.float32)
+    line_sum = line_sum.reshape(32, 8, width)
+    pieces = lax.all_to_all(line_sum.astype(jnp.bfloat16), ("x", "z"), 0, 0)
+    sigma = pieces.astype(jnp.float32).sum(0)
     own_tile = lax.axis_index(("y", "x", "c"))
     own_rows = own_tile * 8 + lax.broadcasted_iota(jnp.int32, (8, 1), 0)
     return jnp.where(own_rows < block_rows[0], sigma, jnp.zeros_like(sigma))[None]

time: 62.8 us -> 61.2 us (0.975)
  blocking collectives: 20.9 us -> 0 us
  starting transfers between devices: 13.9 us -> 25.7 us
  waiting for transfers between devices: 13.6 us -> 20.9 us
    all_to_all x1 -> x0, blocking collectives: 20.9 us -> none  [body(): pieces = lax.all_to_all(pair_sum.astype(jnp.bfloat16), LAYER, 0, 0)]
    ppermute x0 -> x3, starting transfers between devices: none -> 7.5 us  [body(): arrived = lax.ppermute(piece(shift).astype(jnp.bfloat16), 'y', moves)]
    ppermute x0 -> x3, waiting for transfers between devices: none -> 5.2 us  [body(): arrived = lax.ppermute(piece(shift).astype(jnp.bfloat16), 'y', moves)]
    all_to_all x1, starting transfers between devices: 3.82 us -> 8.08 us  [body(): pieces = lax.all_to_all(line_sum.astype(jnp.bfloat16), ('x', 'z'), 0, 0)]
    ppermute x4, waiting for transfers between devices: 2.6 us -> 4.01 us  [fetch(): return lax.ppermute(value, ('c', 'z'), moves)]
    all_to_all x1, waiting for transfers between devices: 8.37 us -> 9.07 us  [body(): pieces = lax.all_to_all(line_sum.astype(jnp.bfloat16), ('x', 'z'), 0, 0)]
    reduce_sum x2 -> x1, other arithmetic: 0.7 us -> 0.04 us  [body(): sigma = pieces.astype(jnp.float32).sum(0)]
  transfers between devices with their start and end apart: 7 -> 10, of which waited for: 5 -> 7; matrix products, arithmetic and copies ran while one was open for 0% -> 0% of each run, Pallas kernels for 11% -> 12%
where the time goes in v4:
time: 61.2 us; the launch traced here: 60.3 us
  starting transfers between devices  25.7 us (42%)
  waiting for transfers between devices  20.9 us (34%)
  Pallas kernels  8.82 us (14%)
  other arithmetic  2.64 us (4%)
  between operations  1.51 us (2%)
  local copies, waits for them, and re-layouts  0.78 us (1%)
    ppermute x4, starting transfers between devices, fetch(): return lax.ppermute(value, ('c', 'z'), moves)  9.93 us
    all_to_all x1, waiting for transfers between devices, body(): pieces = lax.all_to_all(line_sum.astype(jnp.bfloat16), ('x', 'z'), 0, 0)  9.07 us
    all_to_all x1, starting transfers between devices, body(): pieces = lax.all_to_all(line_sum.astype(jnp.bfloat16), ('x', 'z'), 0, 0)  8.08 us
    ppermute x3, starting transfers between devices, body(): arrived = lax.ppermute(piece(shift).astype(jnp.bfloat16), 'y', moves)  7.5 us
    pallas_call x1, Pallas kernels, prepare(): pl.pallas_call(prepare_kernel, out_shape=(jax.ShapeDtypeStruct((3, 3, slo...  5.95 us
    ppermute x3, waiting for transfers between devices, body(): arrived = lax.ppermute(piece(shift).astype(jnp.bfloat16), 'y', moves)  5.2 us
    ppermute x4, waiting for transfers between devices, fetch(): return lax.ppermute(value, ('c', 'z'), moves)  4.01 us
    ppermute x1, waiting for transfers between devices, body(): received = lax.ppermute(send, 'c', SWAP)  1.85 us
  transfers between devices with their start and end apart: 10, of which 7 were waited for; matrix products, arithmetic and copies ran while one was open for 0% of the time, Pallas kernels for 12%

profile of v4, /device:TPU:2, one launch (start us, length us, event | category | flops | bytes accessed | tf_op | source)
XLA Modules:
  0.0 60.3 jit_solution(1114641689712172895)
XLA Ops:
  0.7 1.0 %bitcast_select_fusion.own = bf16[256,256]{1,0:T(8,128)(2,1)S(1)} fusion(bf16[1,256,256]{2,1,0:T(8,128)(2,1)} %param.6, pred[256]{0:T(512)(128)(4,1)S(1)} %iota_compare_fusion), kind=kLoop, calls=%fused_computation.13 | loop fusion | flops 65536 | bytes 262400 | tf_op jit(solution)/shard_map/jit(_where)/select_n | solution.py:222
  1.7 4.7 %collective-permute-start = (bf16[256,256]{1,0:T(8,128)(2,1)S(1)}, bf16[256,256]{1,0:T(8,128)(2,1)S(1)}, u32[]{:S(2)}, u32[]{:S(2)}) collective-permute-start(bf16[256,256]{1,0:T(8,128)(2,1)S(1)} %bitcast_select_fusion.own), channel_id=1, source_target_pairs={{0,3},{1,4},{2,5},{3,6},{4,7},{5,0},{6,1},{7,2},{8,13},{9,14},{10,... | collective-permute-start | bytes 393224 | tf_op jit(solution)/shard_map/ppermute | solution.py:212
  6.4 3.6 %collective-permute-start.1 = (bf16[256,256]{1,0:T(8,128)(2,1)S(1)}, bf16[256,256]{1,0:T(8,128)(2,1)S(1)}, u32[]{:S(2)}, u32[]{:S(2)}) collective-permute-start(bf16[256,256]{1,0:T(8,128)(2,1)S(1)} %bitcast_select_fusion.own), channel_id=1, source_target_pairs={{0,2},{1,3},{2,4},{3,5},{4,6},{5,7},{6,0},{7,1},{8,14},{9,15},{10,... | collective-permute-start | bytes 393224 | tf_op jit(solution)/shard_map/ppermute | solution.py:212
  10.0 1.0 %collective-permute-start.2 = (bf16[256,256]{1,0:T(8,128)(2,1)S(1)}, bf16[256,256]{1,0:T(8,128)(2,1)S(1)}, u32[]{:S(2)}, u32[]{:S(2)}) collective-permute-start(bf16[256,256]{1,0:T(8,128)(2,1)S(1)} %bitcast_select_fusion.own), channel_id=1, source_target_pairs={{0,1},{1,2},{2,3},{3,4},{4,5},{5,6},{6,7},{7,0},{8,15},{9,8},{10,9... | collective-permute-start | bytes 393224 | tf_op jit(solution)/shard_map/ppermute | solution.py:212
  11.0 0.6 %collective-permute-start.3 = (bf16[128,256]{1,0:T(8,128)(2,1)S(1)}, bf16[128,256]{1,0:T(8,128)(2,1)S(1)}, u32[]{:S(2)}, u32[]{:S(2)}) collective-permute-start(bf16[128,256]{1,0:T(8,128)(2,1)S(1)} %slice_select_fusion), channel_id=1, source_target_pairs={{0,4},{1,5},{2,6},{3,7},{4,0},{5,1},{6,2},{7,3},{8,12},{9,13},{10,... | collective-permute-start | bytes 196616 | tf_op jit(solution)/shard_map/ppermute | solution.py:212
  12.4 0.7 %copy-done = s32[48,2]{0,1:T(2,128)S(1)} copy-done((s32[48,2]{0,1:T(2,128)S(1)}, s32[48,2]{0,1:T(2,128)}, u32[]{:S(2)}) %copy-start) | copy-done | bytes 408
  13.0 5.9 %shard_map.64 = (s32[3,3,56]{2,1,0:T(4,128)S(1)}, s32[3]{0:T(128)S(1)}, bf16[48,256,256]{2,1,0:T(8,128)(2,1)S(1)}, bf16[48,256,256]{2,1,0:T(8,128)(2,1)S(1)}, f32[2,16,9,8,256]{4,3,2,1,0:T(8,128)S(1)}) custom-call(s32[2]{0:T(128)S(1)} %pad_add_fusion.place_ref, s32[1]{0:T(128)S(6)} %copy.14.live_ref, s32[2,48]{1,0:T(2,128)S(1)} %bitcast.29, ...), custom_call_target="tpu_custom_call" | custom-call | bytes 25165824 | tf_op jit(solution)/shard_map/pallas_call | solution.py:121
  19.0 4.0 %collective-permute-done.3 = bf16[128,256]{1,0:T(8,128)(2,1)S(1)} collective-permute-done((bf16[128,256]{1,0:T(8,128)(2,1)S(1)}, bf16[128,256]{1,0:T(8,128)(2,1)S(1)}, u32[]{:S(2)}, u32[]{:S(2)}) %collective-permute-start.3) | collective-permute-done | bytes 65568 | tf_op jit(solution)/shard_map/ppermute | solution.py:212
  23.1 0.1 collective-permute-start.4
  23.2 1.1 %shard_map.65.before = f32[2,16,9,8,256]{4,3,2,1,0:T(8,128)S(1)} custom-call(s32[3,3,56]{2,1,0:T(4,128)S(1)} %get-tuple-element.26.lists_ref, s32[3]{0:T(128)S(1)} %get-tuple-element.27.counts_ref, bf16[1024,256]{1,0:T(8,128)(2,1)S(1)} %constant_dynamic-update-slice_fusion.psi.mine, ...), custom_call_target="tpu_custom_call", output_to_operand_aliasing={{}: (5, {})} | custom-call | flops 1610612736 | bytes 6291456 | tf_op jit(solution)/shard_map/pallas_call | solution.py:148
  24.3 0.8 %collective-permute-done.4.other = bf16[1024,256]{1,0:T(8,128)(2,1)S(1)} collective-permute-done((bf16[1024,256]{1,0:T(8,128)(2,1)S(1)}, bf16[1024,256]{1,0:T(8,128)(2,1)S(1)}, u32[]{:S(2)}, u32[]{:S(2)}) %collective-permute-start.4) | collective-permute-done | bytes 524320 | tf_op jit(solution)/shard_map/ppermute | solution.py:230
  25.1 1.7 %shard_map.66 = (f32[16,64,256]{2,1,0:T(8,128)S(1)}, bf16[16,64,256]{2,1,0:T(8,128)(2,1)S(1)}) custom-call(s32[2]{0:T(128)S(1)} %pad_add_fusion.place_ref, s32[3,3,56]{2,1,0:T(4,128)S(1)} %get-tuple-element.26.lists_ref, s32[3]{0:T(128)S(1)} %get-tuple-element.27.counts_ref, bf16[1024,256]{1,0:T(8,128)(2,1)S(1)} %constant_dynamic-update-slice_fusion.psi.mine, ...), custom_call_target="tpu_custom_call" | custom-call | flops 1610612736 | bytes 6291456 | tf_op jit(solution)/shard_map/pallas_call | solution.py:189
  27.0 1.9 %collective-permute-done.5 = bf16[16,64,256]{2,1,0:T(8,128)(2,1)S(1)} collective-permute-done((bf16[16,64,256]{2,1,0:T(8,128)(2,1)S(1)}, bf16[16,64,256]{2,1,0:T(8,128)(2,1)S(1)}, u32[]{:S(2)}, u32[]{:S(2)}) %collective-permute-start.5) | collective-permute-done | bytes 524320 | tf_op jit(solution)/shard_map/ppermute | solution.py:233
  28.8 0.1 convert_add_fusion
  29.0 4.3 %collective-permute-start.6 = (bf16[256,256]{1,0:T(8,128)(2,1)S(1)}, bf16[256,256]{1,0:T(8,128)(2,1)S(1)}, u32[]{:S(2)}, u32[]{:S(2)}) collective-permute-start(bf16[256,256]{1,0:T(8,128)(2,1)S(1)} %get-tuple-element.37), channel_id=1, source_target_pairs={{0,128},{64,192},{128,0},{192,64},{1,129},{65,193},{129,1},{193,65... | collective-permute-start | bytes 393224 | tf_op jit(solution)/shard_map/ppermute | solution.py:243
  33.3 2.1 %collective-permute-start.7 = (bf16[256,256]{1,0:T(8,128)(2,1)S(1)}, bf16[256,256]{1,0:T(8,128)(2,1)S(1)}, u32[]{:S(2)}, u32[]{:S(2)}) collective-permute-start(bf16[256,256]{1,0:T(8,128)(2,1)S(1)} %get-tuple-element.39), channel_id=1, source_target_pairs={{0,64},{64,128},{128,192},{192,0},{1,65},{65,129},{129,193},{193,1... | collective-permute-start | bytes 393224 | tf_op jit(solution)/shard_map/ppermute | solution.py:243
  35.4 1.1 %collective-permute-start.8 = (bf16[256,256]{1,0:T(8,128)(2,1)S(1)}, bf16[256,256]{1,0:T(8,128)(2,1)S(1)}, u32[]{:S(2)}, u32[]{:S(2)}) collective-permute-start(bf16[256,256]{1,0:T(8,128)(2,1)S(1)} %get-tuple-element.38), channel_id=1, source_target_pairs={{0,192},{64,0},{128,64},{192,128},{1,193},{65,1},{129,65},{193,129... | collective-permute-start | bytes 393224 | tf_op jit(solution)/shard_map/ppermute | solution.py:243
  36.5 0.8 %collective-permute-done.6 = bf16[256,256]{1,0:T(8,128)(2,1)S(1)} collective-permute-done((bf16[256,256]{1,0:T(8,128)(2,1)S(1)}, bf16[256,256]{1,0:T(8,128)(2,1)S(1)}, u32[]{:S(2)}, u32[]{:S(2)}) %collective-permute-start.6) | collective-permute-done | bytes 131104 | tf_op jit(solution)/shard_map/ppermute | solution.py:243
  37.3 2.8 %collective-permute-done.7 = bf16[256,256]{1,0:T(8,128)(2,1)S(1)} collective-permute-done((bf16[256,256]{1,0:T(8,128)(2,1)S(1)}, bf16[256,256]{1,0:T(8,128)(2,1)S(1)}, u32[]{:S(2)}, u32[]{:S(2)}) %collective-permute-start.7) | collective-permute-done | bytes 131104 | tf_op jit(solution)/shard_map/ppermute | solution.py:243
  40.1 1.6 %collective-permute-done.8 = bf16[256,256]{1,0:T(8,128)(2,1)S(1)} collective-permute-done((bf16[256,256]{1,0:T(8,128)(2,1)S(1)}, bf16[256,256]{1,0:T(8,128)(2,1)S(1)}, u32[]{:S(2)}, u32[]{:S(2)}) %collective-permute-start.8) | collective-permute-done | bytes 131104 | tf_op jit(solution)/shard_map/ppermute | solution.py:243
  41.7 0.7 %fusion.6 = bf16[32,8,256]{2,1,0:T(8,128)(2,1)} fusion(bf16[256,256]{1,0:T(8,128)(2,1)S(1)} %collective-permute-done.8, bf16[256,256]{1,0:T(8,128)(2,1)S(1)} %collective-permute-done.7, bf16[256,256]{1,0:T(8,128)(2,1)S(1)} %collective-permute-done.6, f32[4,256,256]{2,1,0:T(8,128)S(1)} %bitcast.31, s32[]{:T(128)S(6)} %select_n.59), kind=kLoop, calls=%fused_computation.12 | loop fusion | flops 458752 | bytes 786436 | tf_op jit(solution)/shard_map/convert_element_type | solution.py:246
  42.4 8.1 %all-to-all-start = ((bf16[32,8,256]{2,1,0:T(8,128)(2,1)}), bf16[32,8,256]{2,1,0:T(8,128)(2,1)S(1)}, u32[]{:S(2)}, u32[]{:S(2)}) async-start(bf16[32,8,256]{2,1,0:T(8,128)(2,1)} %fusion.6), calls=%async_computation | async-start | bytes 262144 | tf_op jit(solution)/shard_map/all_to_all | solution.py:246
  50.6 9.1 %all-to-all-done = bf16[32,8,256]{2,1,0:T(8,128)(2,1)S(1)} async-done(((bf16[32,8,256]{2,1,0:T(8,128)(2,1)}), bf16[32,8,256]{2,1,0:T(8,128)(2,1)S(1)}, u32[]{:S(2)}, u32[]{:S(2)}) %all-to-all-start) | async-done | bytes 131104 | tf_op jit(solution)/shard_map/all_to_all | solution.py:246
  59.7 0.7 %bitcast_select_fusion.1 = f32[1,8,256]{2,1,0:T(8,128)} fusion(f32[8,256]{1,0:T(8,128)S(1)} %convert_reduce_fusion, pred[8]{0:T(512)(128)(4,1)S(1)} %add_compare_fusion), kind=kLoop, calls=%fused_computation.20 | loop fusion | flops 2048 | bytes 16392 | tf_op jit(solution)/shard_map/jit(_where)/select_n | solution.py:250
  (16 shorter events, 0.3 us)
Async XLA Ops:
  1.7 21.3 %collective-permute-start = (bf16[256,256]{1,0:T(8,128)(2,1)S(1)}, bf16[256,256]{1,0:T(8,128)(2,1)S(1)}, u32[]{:S(2)}, u32[]{:S(2)}) collective-permute-start(bf16[256,256]{1,0:T(8,128)(2,1)S(1)} %bitcast_select_fusion.own), channel_id=1, source_target_pairs={{0,3},{1,4},{2,5},{3,6},{4,7},{5,0},{6,1},{7,2},{8,13},{9,14},{10,... | collective-permute-start | bytes 393224 | tf_op jit(solution)/shard_map/ppermute | solution.py:212
  6.4 16.6 %collective-permute-start.1 = (bf16[256,256]{1,0:T(8,128)(2,1)S(1)}, bf16[256,256]{1,0:T(8,128)(2,1)S(1)}, u32[]{:S(2)}, u32[]{:S(2)}) collective-permute-start(bf16[256,256]{1,0:T(8,128)(2,1)S(1)} %bitcast_select_fusion.own), channel_id=1, source_target_pairs={{0,2},{1,3},{2,4},{3,5},{4,6},{5,7},{6,0},{7,1},{8,14},{9,15},{10,... | collective-permute-start | bytes 393224 | tf_op jit(solution)/shard_map/ppermute | solution.py:212
  10.0 13.0 %collective-permute-start.2 = (bf16[256,256]{1,0:T(8,128)(2,1)S(1)}, bf16[256,256]{1,0:T(8,128)(2,1)S(1)}, u32[]{:S(2)}, u32[]{:S(2)}) collective-permute-start(bf16[256,256]{1,0:T(8,128)(2,1)S(1)} %bitcast_select_fusion.own), channel_id=1, source_target_pairs={{0,1},{1,2},{2,3},{3,4},{4,5},{5,6},{6,7},{7,0},{8,15},{9,8},{10,9... | collective-permute-start | bytes 393224 | tf_op jit(solution)/shard_map/ppermute | solution.py:212
  11.0 12.0 %collective-permute-start.3 = (bf16[128,256]{1,0:T(8,128)(2,1)S(1)}, bf16[128,256]{1,0:T(8,128)(2,1)S(1)}, u32[]{:S(2)}, u32[]{:S(2)}) collective-permute-start(bf16[128,256]{1,0:T(8,128)(2,1)S(1)} %slice_select_fusion), channel_id=1, source_target_pairs={{0,4},{1,5},{2,6},{3,7},{4,0},{5,1},{6,2},{7,3},{8,12},{9,13},{10,... | collective-permute-start | bytes 196616 | tf_op jit(solution)/shard_map/ppermute | solution.py:212
  12.4 0.7 %copy-start = (s32[48,2]{0,1:T(2,128)S(1)}, s32[48,2]{0,1:T(2,128)}, u32[]{:S(2)}) copy-start(s32[48,2]{0,1:T(2,128)} %param.10) | copy-start | bytes 1156
  23.1 2.0 %collective-permute-start.4 = (bf16[1024,256]{1,0:T(8,128)(2,1)S(1)}, bf16[1024,256]{1,0:T(8,128)(2,1)S(1)}, u32[]{:S(2)}, u32[]{:S(2)}) collective-permute-start(bf16[1024,256]{1,0:T(8,128)(2,1)S(1)} %constant_dynamic-update-slice_fusion.psi.mine), channel_id=1, source_target_pairs={{0,8},{8,0},{1,9},{9,1},{2,10},{10,2},{3,11},{11,3},{4,12},{12,4},... | collective-permute-start | bytes 1572872 | tf_op jit(solution)/shard_map/ppermute | solution.py:230
  26.8 2.0 %collective-permute-start.5 = (bf16[16,64,256]{2,1,0:T(8,128)(2,1)S(1)}, bf16[16,64,256]{2,1,0:T(8,128)(2,1)S(1)}, u32[]{:S(2)}, u32[]{:S(2)}) collective-permute-start(bf16[16,64,256]{2,1,0:T(8,128)(2,1)S(1)} %get-tuple-element.36), channel_id=1, source_target_pairs={{0,8},{8,0},{1,9},{9,1},{2,10},{10,2},{3,11},{11,3},{4,12},{12,4},... | collective-permute-start | bytes 1572872 | tf_op jit(solution)/shard_map/ppermute | solution.py:233
  29.0 8.3 %collective-permute-start.6 = (bf16[256,256]{1,0:T(8,128)(2,1)S(1)}, bf16[256,256]{1,0:T(8,128)(2,1)S(1)}, u32[]{:S(2)}, u32[]{:S(2)}) collective-permute-start(bf16[256,256]{1,0:T(8,128)(2,1)S(1)} %get-tuple-element.37), channel_id=1, source_target_pairs={{0,128},{64,192},{128,0},{192,64},{1,129},{65,193},{129,1},{193,65... | collective-permute-start | bytes 393224 | tf_op jit(solution)/shard_map/ppermute | solution.py:243
  33.3 6.8 %collective-permute-start.7 = (bf16[256,256]{1,0:T(8,128)(2,1)S(1)}, bf16[256,256]{1,0:T(8,128)(2,1)S(1)}, u32[]{:S(2)}, u32[]{:S(2)}) collective-permute-start(bf16[256,256]{1,0:T(8,128)(2,1)S(1)} %get-tuple-element.39), channel_id=1, source_target_pairs={{0,64},{64,128},{128,192},{192,0},{1,65},{65,129},{129,193},{193,1... | collective-permute-start | bytes 393224 | tf_op jit(solution)/shard_map/ppermute | solution.py:243
  35.4 6.3 %collective-permute-start.8 = (bf16[256,256]{1,0:T(8,128)(2,1)S(1)}, bf16[256,256]{1,0:T(8,128)(2,1)S(1)}, u32[]{:S(2)}, u32[]{:S(2)}) collective-permute-start(bf16[256,256]{1,0:T(8,128)(2,1)S(1)} %get-tuple-element.38), channel_id=1, source_target_pairs={{0,192},{64,0},{128,64},{192,128},{1,193},{65,1},{129,65},{193,129... | collective-permute-start | bytes 393224 | tf_op jit(solution)/shard_map/ppermute | solution.py:243
  42.4 17.2 %all-to-all-start = ((bf16[32,8,256]{2,1,0:T(8,128)(2,1)}), bf16[32,8,256]{2,1,0:T(8,128)(2,1)S(1)}, u32[]{:S(2)}, u32[]{:S(2)}) async-start(bf16[32,8,256]{2,1,0:T(8,128)(2,1)} %fusion.6), calls=%async_computation | async-start | bytes 262144 | tf_op jit(solution)/shard_map/all_to_all | solution.py:246
